TPU v7x, 256 devices: a whole 4x4x8 slice. The times are simulated.
256 devices in a mesh: dp: 8 (over x, core), gx: 32 (over z, y).
Axes of the slice: x: 4, y: 4, z: 8, core: 2. Of those that a mesh axis runs over, the one named last changes fastest.
Arguments:
- features: bfloat16 [16, 64, 128, 8, 128], P('dp', None, 'gx'), may hold values from -6 to 6
- labels: int32 [16, 128, 8, 128], P('dp', 'gx'), may hold values from 0 to 7
- embedding: float32 [8, 64], replicated, may hold values from -4 to 4
- weight_one: bfloat16 [3, 3, 3, 64, 64], replicated, may hold values from -0.15625 to 0.15625
- weight_two: bfloat16 [3, 3, 3, 64, 64], replicated, may hold values from -0.15625 to 0.15625
- cotangent: bfloat16 [16, 64, 128, 8, 128], P('dp', None, 'gx'), may hold values from -6 to 6
Outputs:
- output: bfloat16 [16, 64, 128, 8, 128], P('dp', None, 'gx')
- grad_one: float32 [3, 3, 3, 64, 64], replicated
- grad_two: float32 [3, 3, 3, 64, 64], replicated
All inputs are finite; a program needn't handle non-finite values.
Results may differ from a plain program's by a relative error of at most 0.015.
Values may be sent and summed in bfloat16 or wider, within the bound.
A program may use at most 128 MiB of HBM per device.

v0:
```python
import math

import jax
import jax.numpy as jnp
from jax import lax
from jax.sharding import PartitionSpec as P


def extended_2(block, sides, width):
    for axis, dim in sides:
        count = lax.axis_size(axis)
        forward = [(i, i + 1) for i in range(count - 1)]
        forward.append((count - 1, 0))
        backward = [(target, source) for source, target in forward]
        low = lax.ppermute(
            lax.slice_in_dim(block, block.shape[dim] - width, None, axis=dim), axis, forward
        )
        high = lax.ppermute(lax.slice_in_dim(block, 0, width, axis=dim), axis, backward)
        block = jnp.concatenate([low, block, high], axis=dim)
    return block


def convolve(extended, kernel):
    return lax.conv_general_dilated(
        extended,
        kernel,
        (1, 1, 1),
        ((0, 0), (1, 1), (1, 1)),
        dimension_numbers=("NCDHW", "DHWIO", "NCDHW"),
        preferred_element_type=jnp.float32,
    )


def tap_terms(extended, partner):
    padded = jnp.pad(extended, ((0, 0), (0, 0), (0, 0), (1, 1), (1, 1)))
    planes = partner.shape[2]
    depth = partner.shape[3]
    span = partner.shape[4]
    terms = []
    for first in range(3):
        for second in range(3):
            for third in range(3):
                window = padded[
                    :, :, first : first + planes, second : second + depth, third : third + span
                ]
                terms.append(
                    jnp.einsum(
                        "bixzy,boxzy->io", window, partner, preferred_element_type=jnp.float32
                    )
                )
    stacked = jnp.stack(terms)
    return stacked.reshape(3, 3, 3, stacked.shape[1], stacked.shape[2])


def on_device(features, labels, embedding, weight_one, weight_two, cotangent):
    summed = features.astype(jnp.float32)
    for label in range(embedding.shape[0]):
        picked = (labels == label).astype(jnp.float32)[:, None]
        summed = summed + picked * embedding[label][None, :, None, None, None]
    base = summed.astype(jnp.bfloat16)
    base_ext = extended_2(base, (("gx", 2),), 1)
    pre = convolve(base_ext, weight_one)
    hidden = jax.nn.silu(pre).astype(jnp.bfloat16)
    hidden_ext = extended_2(hidden, (("gx", 2),), 1)
    output = (base.astype(jnp.float32) + convolve(hidden_ext, weight_two)).astype(jnp.bfloat16)
    cot_ext = extended_2(cotangent, (("gx", 2),), 1)
    grad_second = tap_terms(hidden_ext, cotangent)
    flipped = jnp.swapaxes(weight_two[::-1, ::-1, ::-1], 3, 4)
    d_hidden = convolve(cot_ext, flipped)
    sig = jax.nn.sigmoid(pre)
    d_pre = (d_hidden * sig * (1.0 + pre * (1.0 - sig))).astype(jnp.bfloat16)
    grad_first = tap_terms(base_ext, d_pre)
    count = (
        features.shape[0]
        * lax.axis_size("dp")
        * features.shape[2]
        * lax.axis_size("gx")
        * features.shape[3]
        * features.shape[4]
    )
    factor = 1.0 / math.sqrt(count)
    total_first, total_second = lax.psum((grad_first, grad_second), ("dp", "gx"))
    return (output, total_first * factor, total_second * factor)


def solution(mesh):
    placed = (
        P("dp", None, "gx", None, None),
        P("dp", "gx", None, None),
        P(),
        P(),
        P(),
        P("dp", None, "gx", None, None),
    )
    return jax.shard_map(
        on_device,
        mesh=mesh,
        in_specs=placed,
        out_specs=(P("dp", None, "gx", None, None), P(), P()),
        check_vma=False,
    )
```

profile of v0, /device:TPU:1, one launch (start us, length us, event | category | flops | bytes accessed | tf_op | source)
XLA Modules:
  0.0 420.4 jit_solution(10495460154054655702)
XLA Ops:
  7.2 2.7 copy.57
  10.1 2.2 collective-permute-start.4
  12.3 6.8 %collective-permute-start.5 = (bf16[2,64,1,8,128]{1,3,4,0,2:T(8,128)(2,1)S(1)}, bf16[2,64,1,8,128]{1,3,4,0,2:T(8,128)(2,1)S(1)}, u32[]{:S(2)}, u32[]{:S(2)}) collective-permute-start(bf16[2,64,1,8,128]{1,3,4,0,2:T(8,128)(2,1)S(1)} %get-tuple-element.14), channel_id=1, source_target_pairs={{1,0},{2,1},{3,2},{4,3},{5,4},{6,5},{7,6},{8,7},{9,8},{10,9},{11,1... | collective-permute-start | bytes 786440 | tf_op jit(solution)/shard_map/ppermute | solution.py:18
  19.3 1.5 add_convert_fusion
  21.0 4.8 %collective-permute-start.1 = (bf16[2,64,1,8,128]{4,1,3,2,0:T(8,128)(2,1)S(1)}, bf16[2,64,1,8,128]{4,1,3,2,0:T(8,128)(2,1)S(1)}, u32[]{:S(2)}, u32[]{:S(2)}) collective-permute-start(bf16[2,64,1,8,128]{4,1,3,2,0:T(8,128)(2,1)S(1)} %get-tuple-element.20), channel_id=1, source_target_pairs={{1,0},{2,1},{3,2},{4,3},{5,4},{6,5},{7,6},{8,7},{9,8},{10,9},{11,1... | collective-permute-start | bytes 786440 | tf_op jit(solution)/shard_map/ppermute | solution.py:18
  25.8 4.9 %collective-permute-done.4 = bf16[2,64,1,8,128]{1,3,4,0,2:T(8,128)(2,1)S(1)} collective-permute-done((bf16[2,64,1,8,128]{1,3,4,0,2:T(8,128)(2,1)S(1)}, bf16[2,64,1,8,128]{1,3,4,0,2:T(8,128)(2,1)S(1)}, u32[]{:S(2)}, u32[]{:S(2)}) %collective-permute-start.4) | collective-permute-done | bytes 262176 | tf_op jit(solution)/shard_map/ppermute | solution.py:15
  30.7 0.7 maximum_bitcast_fusion
  31.4 0.7 pad.13
  32.2 2.7 fusion.5
  34.9 1.3 collective-permute-done
  36.3 1.5 pad_maximum_fusion
  37.8 4.4 %copy.150 = bf16[64,6,8,2,128]{0,2,4,3,1:T(8,128)(2,1)} copy(bf16[64,6,8,2,128]{4,0,2,1,3:T(8,128)(2,1)} %get-tuple-element.18) | data formatting | bytes 3145728
  42.1 2.7 pad.9.clone
  44.8 0.8 fusion.3
  45.6 10.2 %multiply_convert_fusion.1 = (bf16[4,8,16,17,64]{4,2,3,1,0:T(8,128)(2,1)}, f32[4,8,16,17,64]{4,2,3,1,0:T(8,128)S(1)}) fusion(pred[16,17]{0,1:T(8,128)(4,1)S(1)} %copy-done.44, bf16[3,3,3,64,64]{4,3,2,1,0:T(8,128)(2,1)S(1)} %copy-done, bf16[64,6,8,2,8,19]{0,2,5,4,3,1:T(8,128)(2,1)S(1)} %fusion.3), kind=kOutput, calls=%fused_computation.53 | convolution fusion | flops 1768095744 | bytes 5431568 | tf_op jit(solution)/shard_map/conv_general_dilated | solution.py:24
  55.9 17.1 %multiply_convert_fusion = bf16[4,8,16,17,64]{4,2,3,1,0:T(8,128)(2,1)S(1)} fusion(f32[4,8,16,17,64]{4,2,3,1,0:T(8,128)S(1)} %get-tuple-element.38, bf16[3,3,3,64,64]{4,3,2,1,0:T(8,128)(2,1)S(1)} %copy-done.42, bf16[64,6,8,2,8,19]{0,2,5,4,3,1:T(8,128)(2,1)S(1)} %copy-done.8, pred[16,17]{0,1:T(8,128)(4,1)S(1)} %copy-done.44), kind=kOutput, calls=%fused_computation.52 | convolution fusion | flops 1770881024 | bytes 5431568 | tf_op jit(solution)/shard_map/conv_general_dilated | solution.py:24
  73.6 1.5 slice.299
  75.0 2.5 copy.149
  89.9 0.9 copy-done.10
  90.8 1.0 fusion.219
  91.9 0.8 slice.290
  92.8 2.0 copy.145
  94.8 1.2 copy.51
  96.0 0.8 slice.293
  96.8 2.0 copy.147
  98.9 4.8 %collective-permute-start.3 = (bf16[2,64,1,8,128]{4,1,3,2,0:T(8,128)(2,1)}, bf16[2,64,1,8,128]{4,1,3,2,0:T(8,128)(2,1)S(1)}, u32[]{:S(2)}, u32[]{:S(2)}) collective-permute-start(bf16[2,64,1,8,128]{4,1,3,2,0:T(8,128)(2,1)} %bitcast.563), channel_id=1, source_target_pairs={{1,0},{2,1},{3,2},{4,3},{5,4},{6,5},{7,6},{8,7},{9,8},{10,9},{11,1... | collective-permute-start | bytes 786440 | tf_op jit(solution)/shard_map/ppermute | solution.py:18
  103.6 1.0 fusion.86
  105.2 1.5 slice.291
  106.7 3.4 copy.146
  110.2 1.1 fusion.85
  113.2 0.7 fusion.83
  115.2 0.8 fusion.45
  117.2 0.7 fusion.78
  121.1 0.7 fusion.72
  123.1 0.7 fusion.69
  125.1 0.7 fusion.66
  127.0 0.9 fusion.39
  130.5 3.1 copy.151
  133.6 2.7 pad.11.clone
  136.3 0.8 fusion.4
  137.3 8.6 %broadcast_select_fusion = f32[4,8,16,17,64]{4,2,3,1,0:T(8,128)S(1)} fusion(pred[16,17]{0,1:T(8,128)(4,1)S(1)} %copy-done.45, bf16[3,3,3,64,64]{4,3,2,1,0:T(8,128)(2,1)S(1)} %copy-done.43, bf16[64,6,8,2,8,19]{0,2,5,4,3,1:T(8,128)(2,1)S(1)} %fusion.4), kind=kOutput, calls=%fused_computation.68 | convolution fusion | flops 1765310464 | bytes 4317456 | tf_op jit(solution)/shard_map/conv_general_dilated | solution.py:24
  145.9 1.4 copy.55
  147.3 2.3 slice.295
  149.6 3.1 copy.148
  152.9 2.7 fusion.17
  155.6 1.6 copy.90
  157.2 253.1 %all-reduce.5.cloned.1.call-done = (f32[3,3,3,64,64]{4,3,2,1,0:T(8,128)}, f32[3,3,3,64,64]{4,3,2,1,0:T(8,128)}) async-done(((f32[3,3,3,64,64]{4,3,2,1,0:T(8,128)}, f32[3,3,3,64,64]{4,3,2,1,0:T(8,128)}), (f32[3,3,3,64,64]{4,3,2,1,0:T(8,128)}, f32[3,3,3,64,64]{4,3,2,1,0:T(8,128)})) %all-reduce.5.cloned.1.call-update) | async-done | bytes 884752 | tf_op jit(solution)/shard_map/psum | solution.py:82
  410.3 2.9 broadcast_multiply_fusion
  (155 shorter events, 27.9 us)
Async XLA Ops:
  7.2 38.4 %copy-start = (bf16[3,3,3,64,64]{4,3,2,1,0:T(8,128)(2,1)S(1)}, bf16[3,3,3,64,64]{4,3,2,1,0:T(8,128)(2,1)}, u32[]{:S(2)}) copy-start(bf16[3,3,3,64,64]{4,3,2,1,0:T(8,128)(2,1)} %param.9) | copy-start | bytes 663556
  7.2 11.9 %copy-start.41 = (f32[8,64]{1,0:T(8,128)S(1)}, f32[8,64]{1,0:T(8,128)}, u32[]{:S(2)}) copy-start(f32[8,64]{1,0:T(8,128)} %param.8) | copy-start | bytes 6148
  7.2 11.9 %copy-start.24 = (s32[2,4,8,128]{3,2,1,0:T(8,128)S(1)}, s32[2,4,8,128]{3,2,1,0:T(8,128)}, u32[]{:S(2)}) copy-start(s32[2,4,8,128]{3,2,1,0:T(8,128)} %param.7) | copy-start | bytes 98308
  7.2 403.1 %all-reduce.5.cloned.1.call-start = ((), (), s32[]{:S(2)}) async-start(), calls=%async_computation | async-start | bytes 3538944 | tf_op jit(solution)/shard_map/psum | solution.py:82
  10.0 9.3 %copy-start.6 = (bf16[2,64,4,8,128]{4,3,2,1,0:T(8,128)(2,1)S(1)}, bf16[2,64,4,8,128]{4,3,2,1,0:T(8,128)(2,1)}, u32[]{:S(2)}) copy-start(bf16[2,64,4,8,128]{4,3,2,1,0:T(8,128)(2,1)} %param.6) | copy-start | bytes 3145732
  10.1 20.6 %collective-permute-start.4 = (bf16[2,64,1,8,128]{1,3,4,0,2:T(8,128)(2,1)S(1)}, bf16[2,64,1,8,128]{1,3,4,0,2:T(8,128)(2,1)S(1)}, u32[]{:S(2)}, u32[]{:S(2)}) collective-permute-start(bf16[2,64,1,8,128]{1,3,4,0,2:T(8,128)(2,1)S(1)} %get-tuple-element.13), channel_id=1, source_target_pairs={{0,1},{1,2},{2,3},{3,4},{4,5},{5,6},{6,7},{7,8},{8,9},{9,10},{10,1... | collective-permute-start | bytes 786440 | tf_op jit(solution)/shard_map/ppermute | solution.py:15
  12.3 18.4 %collective-permute-start.5 = (bf16[2,64,1,8,128]{1,3,4,0,2:T(8,128)(2,1)S(1)}, bf16[2,64,1,8,128]{1,3,4,0,2:T(8,128)(2,1)S(1)}, u32[]{:S(2)}, u32[]{:S(2)}) collective-permute-start(bf16[2,64,1,8,128]{1,3,4,0,2:T(8,128)(2,1)S(1)} %get-tuple-element.14), channel_id=1, source_target_pairs={{1,0},{2,1},{3,2},{4,3},{5,4},{6,5},{7,6},{8,7},{9,8},{10,9},{11,1... | collective-permute-start | bytes 786440 | tf_op jit(solution)/shard_map/ppermute | solution.py:18
  19.1 1.7 copy-start.25
  19.1 1.7 copy-start.27
  19.1 1.7 copy-start.29
  19.2 1.7 copy-start.31
  19.2 1.7 copy-start.33
  19.2 1.7 copy-start.35
  19.2 1.7 copy-start.37
  19.2 1.7 copy-start.39
  19.2 12.2 %copy-start.12 = (f32[2,4,8,128]{3,2,1,0:T(8,128)}, f32[2,4,8,128]{3,2,1,0:T(8,128)S(1)}, u32[]{:S(2)}) copy-start(f32[2,4,8,128]{3,2,1,0:T(8,128)S(1)} %get-tuple-element.25) | copy-start | bytes 98308
  19.2 12.2 %copy-start.14 = (f32[2,4,8,128]{3,2,1,0:T(8,128)}, f32[2,4,8,128]{3,2,1,0:T(8,128)S(1)}, u32[]{:S(2)}) copy-start(f32[2,4,8,128]{3,2,1,0:T(8,128)S(1)} %get-tuple-element.26) | copy-start | bytes 98308
  19.3 12.2 %copy-start.16 = (f32[2,4,8,128]{3,2,1,0:T(8,128)}, f32[2,4,8,128]{3,2,1,0:T(8,128)S(1)}, u32[]{:S(2)}) copy-start(f32[2,4,8,128]{3,2,1,0:T(8,128)S(1)} %get-tuple-element.27) | copy-start | bytes 98308
  19.3 12.2 %copy-start.18 = (f32[2,4,8,128]{3,2,1,0:T(8,128)}, f32[2,4,8,128]{3,2,1,0:T(8,128)S(1)}, u32[]{:S(2)}) copy-start(f32[2,4,8,128]{3,2,1,0:T(8,128)S(1)} %get-tuple-element.28) | copy-start | bytes 98308
  20.8 15.5 %copy-start.2 = (bf16[2,64,4,8,128]{4,1,3,2,0:T(8,128)(2,1)}, bf16[2,64,4,8,128]{4,1,3,2,0:T(8,128)(2,1)S(1)}, u32[]{:S(2)}) copy-start(bf16[2,64,4,8,128]{4,1,3,2,0:T(8,128)(2,1)S(1)} %add_convert_fusion) | copy-start | bytes 3145732
  20.9 15.4 %collective-permute-start = (bf16[2,64,1,8,128]{4,1,3,2,0:T(8,128)(2,1)S(1)}, bf16[2,64,1,8,128]{4,1,3,2,0:T(8,128)(2,1)S(1)}, u32[]{:S(2)}, u32[]{:S(2)}) collective-permute-start(bf16[2,64,1,8,128]{4,1,3,2,0:T(8,128)(2,1)S(1)} %get-tuple-element.19), channel_id=1, source_target_pairs={{0,1},{1,2},{2,3},{3,4},{4,5},{5,6},{6,7},{7,8},{8,9},{9,10},{10,1... | collective-permute-start | bytes 786440 | tf_op jit(solution)/shard_map/ppermute | solution.py:15
  21.0 15.3 %collective-permute-start.1 = (bf16[2,64,1,8,128]{4,1,3,2,0:T(8,128)(2,1)S(1)}, bf16[2,64,1,8,128]{4,1,3,2,0:T(8,128)(2,1)S(1)}, u32[]{:S(2)}, u32[]{:S(2)}) collective-permute-start(bf16[2,64,1,8,128]{4,1,3,2,0:T(8,128)(2,1)S(1)} %get-tuple-element.20), channel_id=1, source_target_pairs={{1,0},{2,1},{3,2},{4,3},{5,4},{6,5},{7,6},{8,7},{9,8},{10,9},{11,1... | collective-permute-start | bytes 786440 | tf_op jit(solution)/shard_map/ppermute | solution.py:18
  36.3 1.5 copy-start.20
  45.6 10.3 %copy-start.8 = (bf16[64,6,8,2,8,19]{0,2,5,4,3,1:T(8,128)(2,1)S(1)}, bf16[64,6,8,2,8,19]{0,2,5,4,3,1:T(8,128)(2,1)}, u32[]{:S(2)}) copy-start(bf16[64,6,8,2,8,19]{0,2,5,4,3,1:T(8,128)(2,1)} %fusion.5) | copy-start | bytes 5603332
  45.6 10.2 %copy-start.42 = (bf16[3,3,3,64,64]{4,3,2,1,0:T(8,128)(2,1)S(1)}, bf16[3,3,3,64,64]{4,3,2,1,0:T(8,128)(2,1)}, u32[]{:S(2)}) copy-start(bf16[3,3,3,64,64]{4,3,2,1,0:T(8,128)(2,1)} %param.10) | copy-start | bytes 663556
  78.5 1.2 copy-start.3
  78.5 1.3 copy-start.21
  88.8 2.0 copy-start.4
  94.8 16.5 %collective-permute-start.2 = (bf16[2,64,1,8,128]{4,1,3,2,0:T(8,128)(2,1)}, bf16[2,64,1,8,128]{4,1,3,2,0:T(8,128)(2,1)S(1)}, u32[]{:S(2)}, u32[]{:S(2)}) collective-permute-start(bf16[2,64,1,8,128]{4,1,3,2,0:T(8,128)(2,1)} %bitcast.12), channel_id=1, source_target_pairs={{0,1},{1,2},{2,3},{3,4},{4,5},{5,6},{6,7},{7,8},{8,9},{9,10},{10,1... | collective-permute-start | bytes 786440 | tf_op jit(solution)/shard_map/ppermute | solution.py:15
  98.8 5.8 %copy-start.5 = (bf16[4,8,16,17,64]{4,2,3,1,0:T(8,128)(2,1)S(1)}, bf16[4,8,16,17,64]{4,2,3,1,0:T(8,128)(2,1)}, u32[]{:S(2)}) copy-start(bf16[4,8,16,17,64]{4,2,3,1,0:T(8,128)(2,1)} %get-tuple-element.37) | copy-start | bytes 3342340
  98.9 12.5 %collective-permute-start.3 = (bf16[2,64,1,8,128]{4,1,3,2,0:T(8,128)(2,1)}, bf16[2,64,1,8,128]{4,1,3,2,0:T(8,128)(2,1)S(1)}, u32[]{:S(2)}, u32[]{:S(2)}) collective-permute-start(bf16[2,64,1,8,128]{4,1,3,2,0:T(8,128)(2,1)} %bitcast.563), channel_id=1, source_target_pairs={{1,0},{2,1},{3,2},{4,3},{5,4},{6,5},{7,6},{8,7},{9,8},{10,9},{11,1... | collective-permute-start | bytes 786440 | tf_op jit(solution)/shard_map/ppermute | solution.py:18
  110.2 1.2 copy-start.7
  111.4 1.2 copy-start.9
  114.0 1.3 copy-start.23
  130.5 3.1 copy-start.11
  149.6 3.2 copy-start.13
  149.6 3.2 copy-start.15
  149.6 3.2 copy-start.17
  149.6 3.2 copy-start.19
  149.6 3.2 copy-start.26
  149.6 3.2 copy-start.28
  149.6 3.2 copy-start.30
  149.6 3.2 copy-start.32
  149.6 3.2 copy-start.34
  149.6 3.2 copy-start.36
  149.6 3.2 copy-start.38
  149.6 3.2 copy-start.40
  155.6 257.7 %copy-start.1 = (bf16[3,3,3,64,64]{4,3,2,1,0:T(8,128)(2,1)S(1)}, bf16[3,3,3,64,64]{4,3,2,1,0:T(8,128)(2,1)}, u32[]{:S(2)}) copy-start(bf16[3,3,3,64,64]{4,3,2,1,0:T(8,128)(2,1)} %param.9) | copy-start | bytes 663556
  (5 other events, 4.4 us)
Sparse Core Ops, SparseCore 0:
  152.9 257.4 all-reduce.4
where the time goes:
time: 427 us; the launch traced here: 420 us
  waiting for transfers between devices  259 us (61%)
  matrix products  67.6 us (16%)
  local copies, waits for them, and re-layouts  45.5 us (11%)
  starting transfers between devices  18.7 us (4%)
  between operations  15.4 us (4%)
  other arithmetic  13.8 us (3%)
    psum x1, waiting for transfers between devices, on_device(): lax.psum((grad_first, grad_second), ('dp', 'gx'))  253 us
    conv_general_dilated x3, matrix products, convolve(): lax.conv_general_dilated(extended, kernel, (1, 1, 1), ((0, 0), (1, 1), (1...  35.9 us
    dot_general x54, matrix products, tap_terms(): jnp.einsum('bixzy,boxzy->io', window, partner, preferred_element_type=jnp...  31.7 us
    unnamed x101, local copies, waits for them, and re-layouts  27.5 us
    ppermute x3, starting transfers between devices, extended_2(): lax.ppermute(lax.slice_in_dim(block, 0, width, axis=dim), axis, backward)  16.4 us
  transfers between devices with their start and end apart: 7, of which 3 were waited for; matrix products, arithmetic and copies ran while one was open for 5% of the time, Pallas kernels for 0%

commit v1 on v0

v1 whole, which is shorter than its diff:
```python
import functools
import math

import jax
import jax.numpy as jnp
from jax import lax
from jax.experimental import pallas as pl
from jax.experimental.pallas import tpu as pltpu
from jax.sharding import PartitionSpec as P

MESH = pl.DeviceIdType.MESH
F32 = jnp.float32
BF16 = jnp.bfloat16

CH = 64
PLANES = 4
DEPTH = 8
SPAN = 128
CELLS = DEPTH * SPAN
PADDED = CELLS + 2 * SPAN
TRIPLE = 3 * CH
SAMPLES = 2
PACKED = 1024
Y_RING = 4
NT = (((1,), (1,)), ((), ()))


def rows(start, size, unit=16):
    return pl.ds(pl.multiple_of(start, unit), size)


def shifted(value):
    lane = lax.broadcasted_iota(jnp.int32, value.shape, 1)
    after = jnp.where(lane == 0, 0.0, pltpu.roll(value, 1, 1))
    before = jnp.where(lane == SPAN - 1, 0.0, pltpu.roll(value, SPAN - 1, 1))
    return before, after


def body(
    dp_count,
    z_count,
    scale,
    feat_hbm,
    labels_hbm,
    emb_hbm,
    one_hbm,
    two_hbm,
    cot_hbm,
    out_hbm,
    grad_one_ref,
    grad_two_ref,
    feat,
    cot,
    labels,
    emb,
    one,
    two,
    wide,
    base3,
    cot3,
    hid3,
    dpre3,
    factor,
    part,
    w_one,
    w_two,
    w_back,
    acc,
    packed,
    got_dp,
    mine_y,
    got_y,
    all_z,
    full,
    in_sem,
    out_sem,
    halo_send,
    halo_recv,
    dp_send,
    dp_recv,
    y_send,
    y_recv,
    z_send,
    z_recv,
    yg_send,
    yg_recv,
    dg_send,
    dg_recv,
):
    me_dp = lax.axis_index("dp")
    me_gx = lax.axis_index("gx")
    gx_count = z_count * Y_RING
    me_z = me_gx // Y_RING
    me_y = me_gx % Y_RING
    left = (me_dp, (me_gx + gx_count - 1) % gx_count)
    right = (me_dp, (me_gx + 1) % gx_count)

    def dp_peer(k):
        return ((me_dp + k) % dp_count, me_gx)

    def y_peer(k):
        return (me_dp, me_z * Y_RING + (me_y + k) % Y_RING)

    def z_peer(k):
        return (me_dp, ((me_z + k) % z_count) * Y_RING + me_y)

    loads = []
    for at, (src, dst) in enumerate(
        (
            (emb_hbm, emb),
            (labels_hbm, labels),
            (feat_hbm.at[0], feat.at[0]),
            (feat_hbm.at[1], feat.at[1]),
            (cot_hbm.at[0], cot.at[0]),
            (cot_hbm.at[1], cot.at[1]),
            (one_hbm, one),
            (two_hbm, two),
        )
    ):
        copy = pltpu.make_async_copy(src, dst, in_sem.at[at])
        copy.start()
        loads.append(copy)

    for field in (base3, hid3):
        for s in range(SAMPLES):
            for plane in range(PLANES + 2):
                low = plane * TRIPLE + CH
                field[s, low : low + CH, 0:SPAN] = jnp.zeros((CH, SPAN), BF16)
                field[s, low : low + CH, PADDED - SPAN : PADDED] = jnp.zeros((CH, SPAN), BF16)
    part[:, 0:SPAN] = jnp.zeros((TRIPLE, SPAN), F32)
    part[:, PADDED - SPAN : PADDED] = jnp.zeros((TRIPLE, SPAN), F32)

    barrier = pltpu.get_barrier_semaphore()
    peers = [left, right]
    peers += [dp_peer(k) for k in range(1, dp_count)]
    peers += [y_peer(k) for k in range(1, Y_RING)]
    peers += [z_peer(k) for k in range(1, z_count)]
    for peer in peers:
        pl.semaphore_signal(barrier, inc=1, device_id=peer, device_id_type=MESH)

    eye = (
        lax.broadcasted_iota(jnp.int32, (CH, CH), 0) == lax.broadcasted_iota(jnp.int32, (CH, CH), 1)
    ).astype(BF16)
    loads[0].wait()
    loads[1].wait()
    table = emb[...]
    high = table.astype(BF16)
    rest = table - high.astype(F32)
    middle = rest.astype(BF16)
    low = (rest - middle.astype(F32)).astype(BF16)
    pieces = jnp.concatenate(
        [high.astype(F32), middle.astype(F32), low.astype(F32), jnp.zeros((8, CH), F32)], axis=0
    ).astype(BF16)
    turned = lax.dot_general(eye, pieces, NT, preferred_element_type=F32).astype(BF16)

    def widen(source, s):
        def step(c, carry):
            block = source[s, pl.ds(c * 8, 8)].reshape(8 * PLANES * DEPTH, SPAN)
            wide[s, rows(c * 8 * PLANES * DEPTH, 8 * PLANES * DEPTH), :] = block.astype(F32)
            return carry

        lax.fori_loop(0, CH // 8, step, 0)

    def put(field, s, plane, z, value, order):
        before, after = shifted(value)
        first, last = (after, before) if order > 0 else (before, after)
        low = plane * TRIPLE
        lanes = slice((z + 1) * SPAN, (z + 2) * SPAN)
        field[s, rows(low, CH), lanes] = first.astype(BF16)
        field[s, rows(low + CH, CH), lanes] = value.astype(BF16)
        field[s, rows(low + 2 * CH, CH), lanes] = last.astype(BF16)

    def base_plane(s, x):
        kind = lax.broadcasted_iota(jnp.int32, (32, SPAN), 0) % 8
        for z in range(DEPTH):
            row = labels[s, x, z : z + 1, :]
            hot = (jnp.broadcast_to(row, (32, SPAN)) == kind).astype(F32).astype(BF16)
            looked = jnp.dot(turned, hot, preferred_element_type=F32)
            own = wide[s, pl.ds(x * DEPTH + z, CH, stride=PLANES * DEPTH), :]
            put(base3, s, x + 1, z, own + looked, 1)

    def cot_plane(s, x):
        for z in range(DEPTH):
            own = wide[s, pl.ds(x * DEPTH + z, CH, stride=PLANES * DEPTH), :]
            put(cot3, s, x + 1, z, own, -1)

    def halo(field, which, s):
        inner = slice(SPAN, SPAN + CELLS)
        copies = []
        for side, (at, to, device) in enumerate(
            ((1, PLANES + 1, left), (PLANES, 0, right))
        ):
            copies.append(
                pltpu.make_async_remote_copy(
                    src_ref=field.at[s, at * TRIPLE + CH : at * TRIPLE + 2 * CH, inner],
                    dst_ref=field.at[s, to * TRIPLE + CH : to * TRIPLE + 2 * CH, inner],
                    send_sem=halo_send.at[which, s, side],
                    recv_sem=halo_recv.at[which, s, side],
                    device_id=device,
                    device_id_type=MESH,
                )
            )
        return copies

    def halo_shifts(field, s, order):
        def step(side, carry):
            plane = side * (PLANES + 1)
            for z in range(DEPTH):
                lanes = slice((z + 1) * SPAN, (z + 2) * SPAN)
                value = field[s, rows(plane * TRIPLE + CH, CH), lanes].astype(F32)
                before, after = shifted(value)
                first, last = (after, before) if order > 0 else (before, after)
                field[s, rows(plane * TRIPLE, CH), lanes] = first.astype(BF16)
                field[s, rows(plane * TRIPLE + 2 * CH, CH), lanes] = last.astype(BF16)
            return carry

        lax.fori_loop(0, 2, step, 0)

    halos = [[halo(field, which, s) for s in range(SAMPLES)] for which, field in enumerate((base3, cot3, hid3))]

    for s in range(SAMPLES):
        loads[2 + s].wait()
        widen(feat, s)

        def plane_step(x, carry, s=s):
            base_plane(s, x)
            return carry

        lax.fori_loop(0, PLANES, plane_step, 0)
        if s == 0:
            pl.semaphore_wait(barrier, len(peers))
        for copy in halos[0][s]:
            copy.start()
    for s in range(SAMPLES):
        loads[4 + s].wait()
        widen(cot, s)

        def plane_step(x, carry, s=s):
            cot_plane(s, x)
            return carry

        lax.fori_loop(0, PLANES, plane_step, 0)
        for copy in halos[1][s]:
            copy.start()

    loads[6].wait()
    loads[7].wait()
    for b in range(3):
        for source, target in ((one, w_one), (two, w_two)):
            stacked = jnp.concatenate(
                [source[(a * 3 + b) * 3 + e] for a in range(3) for e in range(3)], axis=0
            )
            target[b * CH : (b + 1) * CH, :] = lax.dot_general(
                eye, stacked, NT, preferred_element_type=F32
            ).astype(BF16)
        flat = jnp.concatenate(
            [
                lax.dot_general(
                    eye, two[((2 - a) * 3 + b) * 3 + e], NT, preferred_element_type=F32
                ).astype(BF16)
                for a in range(3)
                for e in range(3)
            ],
            axis=0,
        )
        w_back[b * CH : (b + 1) * CH, :] = lax.dot_general(
            eye, flat, NT, preferred_element_type=F32
        ).astype(BF16)

    def products(field, weights, s, x):
        part[:, SPAN : SPAN + CELLS] = jnp.dot(
            weights[...],
            field[s, rows(x * TRIPLE, 3 * TRIPLE), SPAN : SPAN + CELLS],
            preferred_element_type=F32,
        )

    def summed(z, order):
        total = part[CH : 2 * CH, (z + 1) * SPAN : (z + 2) * SPAN]
        total = total + part[0:CH, (z + 1 - order) * SPAN : (z + 2 - order) * SPAN]
        return total + part[2 * CH :, (z + 1 + order) * SPAN : (z + 2 + order) * SPAN]

    def first_layer(s, x):
        products(base3, w_one, s, x)
        for z in range(DEPTH):
            pre = summed(z, 1)
            q = jax.nn.sigmoid(pre)
            factor[s, x, :, z * SPAN : (z + 1) * SPAN] = q * (1.0 + pre * (1.0 - q))
            put(hid3, s, x + 1, z, pre * q, 1)

    def backward(s, x):
        products(cot3, w_back, s, x)
        for z in range(DEPTH):
            d_pre = summed(z, -1) * factor[s, x, :, z * SPAN : (z + 1) * SPAN]
            before, after = shifted(d_pre)
            lanes = slice(z * SPAN, (z + 1) * SPAN)
            low = x * TRIPLE
            dpre3[s, rows(low, CH), lanes] = before.astype(BF16)
            dpre3[s, rows(low + CH, CH), lanes] = d_pre.astype(BF16)
            dpre3[s, rows(low + 2 * CH, CH), lanes] = after.astype(BF16)

    def second_layer(s, x):
        products(hid3, w_two, s, x)
        for z in range(DEPTH):
            own = base3[s, rows((x + 1) * TRIPLE + CH, CH), (z + 1) * SPAN : (z + 2) * SPAN]
            wide[s, pl.ds(x * DEPTH + z, CH, stride=PLANES * DEPTH), :] = summed(z, 1) + own.astype(F32)

    def inner_planes(work):
        def step(i, carry):
            work(i // 2, 1 + i % 2)
            return carry

        lax.fori_loop(0, 4, step, 0)

    def edge_planes(work, s):
        def step(i, carry):
            work(s, 3 * i)
            return carry

        lax.fori_loop(0, 2, step, 0)

    inner_planes(first_layer)
    for s in range(SAMPLES):
        for copy in halos[0][s]:
            copy.wait_recv()
        halo_shifts(base3, s, 1)
        edge_planes(first_layer, s)
        for copy in halos[2][s]:
            copy.start()
    inner_planes(backward)
    for s in range(SAMPLES):
        for copy in halos[1][s]:
            copy.wait_recv()
        halo_shifts(cot3, s, -1)
        edge_planes(backward, s)

    def gradient(g, field, partner, partner_plane, partner_lane):
        acc[...] = jnp.zeros_like(acc)

        def step(i, carry):
            s = i // PLANES
            x = i % PLANES
            taps = jnp.concatenate(
                [
                    field[s, rows((x + a) * TRIPLE + CH, CH), b * SPAN : b * SPAN + CELLS]
                    for a in range(3)
                    for b in range(3)
                ],
                axis=0,
            )
            other = partner[
                s, rows((x + partner_plane) * TRIPLE, TRIPLE), partner_lane : partner_lane + CELLS
            ]
            acc[...] += lax.dot_general(taps, other, NT, preferred_element_type=F32)
            return carry

        lax.fori_loop(0, SAMPLES * PLANES, step, 0)
        half = 9 * CH // 2
        packed[g, 0 : 9 * CH, :] = acc[:, 0:SPAN].astype(BF16)
        packed[g, 9 * CH : 9 * CH + half, :] = jnp.concatenate(
            [acc[0:half, SPAN:TRIPLE], acc[half : 2 * half, SPAN:TRIPLE]], axis=1
        ).astype(BF16)
        packed[g, 9 * CH + half :, :] = jnp.zeros((PACKED - 9 * CH - half, SPAN), BF16)

    dp_rows = PACKED // dp_count
    y_rows = dp_rows // Y_RING

    def sum_dp(g):
        return [
            pltpu.make_async_remote_copy(
                src_ref=packed.at[g, rows(((me_dp + k) % dp_count) * dp_rows, dp_rows)],
                dst_ref=got_dp.at[g, k - 1],
                send_sem=dp_send.at[g, k - 1],
                recv_sem=dp_recv.at[g, k - 1],
                device_id=dp_peer(k),
                device_id_type=MESH,
            )
            for k in range(1, dp_count)
        ]

    def sum_y(g):
        return [
            pltpu.make_async_remote_copy(
                src_ref=mine_y.at[g, rows(((me_y + k) % Y_RING) * y_rows, y_rows)],
                dst_ref=got_y.at[g, k - 1],
                send_sem=y_send.at[g, k - 1],
                recv_sem=y_recv.at[g, k - 1],
                device_id=y_peer(k),
                device_id_type=MESH,
            )
            for k in range(1, Y_RING)
        ]

    def spread_z(g):
        return [
            pltpu.make_async_remote_copy(
                src_ref=all_z.at[g, me_z],
                dst_ref=all_z.at[g, me_z],
                send_sem=z_send.at[g, k - 1],
                recv_sem=z_recv.at[g, k - 1],
                device_id=z_peer(k),
                device_id_type=MESH,
            )
            for k in range(1, z_count)
        ]

    def my_y_rows():
        return rows(me_dp * dp_rows + me_y * y_rows, y_rows)

    def my_dp_rows():
        return rows(me_dp * dp_rows, dp_rows)

    def gather_y(g):
        return [
            pltpu.make_async_remote_copy(
                src_ref=full.at[g, my_y_rows()],
                dst_ref=full.at[g, my_y_rows()],
                send_sem=yg_send.at[g, k - 1],
                recv_sem=yg_recv.at[g, k - 1],
                device_id=y_peer(k),
                device_id_type=MESH,
            )
            for k in range(1, Y_RING)
        ]

    def gather_dp(g):
        return [
            pltpu.make_async_remote_copy(
                src_ref=full.at[g, my_dp_rows()],
                dst_ref=full.at[g, my_dp_rows()],
                send_sem=dg_send.at[g, k - 1],
                recv_sem=dg_recv.at[g, k - 1],
                device_id=dp_peer(k),
                device_id_type=MESH,
            )
            for k in range(1, dp_count)
        ]

    sent = []

    def start(copies):
        for copy in copies:
            copy.start()
        sent.extend(copies)
        return copies

    def arrived(copies):
        for copy in copies:
            copy.wait_recv()

    def stage_one(g, dp_copies):
        arrived(dp_copies)
        total = packed[g, my_dp_rows(), :].astype(F32)
        for k in range(dp_count - 1):
            total = total + got_dp[g, k].astype(F32)
        mine_y[g] = total.astype(BF16)
        return start(sum_y(g))

    def stage_two(g, y_copies):
        arrived(y_copies)
        total = mine_y[g, rows(me_y * y_rows, y_rows), :].astype(F32)
        for k in range(Y_RING - 1):
            total = total + got_y[g, k].astype(F32)
        all_z[g, me_z] = total.astype(BF16)
        return start(spread_z(g))

    def stage_three(g, z_copies):
        arrived(z_copies)
        total = all_z[g, 0].astype(F32)
        for k in range(1, z_count):
            total = total + all_z[g, k].astype(F32)
        full[g, my_y_rows(), :] = (total * scale).astype(BF16)
        return start(gather_y(g))

    def stage_four(g, yg_copies):
        arrived(yg_copies)
        return start(gather_dp(g))

    def stage_five(g, dg_copies, target):
        arrived(dg_copies)
        half = 9 * CH // 2
        for tap in range(9):
            block = full[g, tap * CH : (tap + 1) * CH, :].astype(F32)
            target[tap * 3] = block[:, 0:CH]
            target[tap * 3 + 1] = block[:, CH:]
        for piece in range(18):
            low = piece * 32
            lane = 0
            if low >= half:
                low, lane = low - half, CH
            block = full[g, 9 * CH + low : 9 * CH + low + 32, lane : lane + CH].astype(F32)
            target[(piece // 2) * 3 + 2, (piece % 2) * 32 : (piece % 2) * 32 + 32, :] = block

    gradient(0, base3, dpre3, 0, 0)
    wait_zero = start(sum_dp(0))
    for s in range(SAMPLES):
        for copy in halos[2][s]:
            copy.wait_recv()
        halo_shifts(hid3, s, 1)
    gradient(1, hid3, cot3, 1, SPAN)
    wait_one = start(sum_dp(1))
    wait_zero = stage_one(0, wait_zero)

    def two_planes(s, first):
        def step(i, carry):
            second_layer(s, first + i)
            return carry

        lax.fori_loop(0, 2, step, 0)

    def give_back(s):
        def step(c, carry):
            block = wide[s, rows(c * 8 * PLANES * DEPTH, 8 * PLANES * DEPTH), :]
            feat[s, pl.ds(c * 8, 8)] = block.reshape(8, PLANES * DEPTH, SPAN).astype(BF16)
            return carry

        lax.fori_loop(0, CH // 8, step, 0)
        copy = pltpu.make_async_copy(feat.at[s], out_hbm.at[s], out_sem.at[s])
        copy.start()
        return copy

    two_planes(0, 0)
    wait_one = stage_one(1, wait_one)
    wait_zero = stage_two(0, wait_zero)
    two_planes(0, 2)
    wait_one = stage_two(1, wait_one)
    wait_zero = stage_three(0, wait_zero)
    out_zero = give_back(0)
    two_planes(1, 0)
    wait_one = stage_three(1, wait_one)
    wait_zero = stage_four(0, wait_zero)
    two_planes(1, 2)
    wait_one = stage_four(1, wait_one)
    out_one = give_back(1)
    stage_five(0, wait_zero, grad_one_ref)
    stage_five(1, wait_one, grad_two_ref)

    out_zero.wait()
    out_one.wait()
    for field in halos:
        for side in field:
            for copy in side:
                copy.wait_send()
    for copy in sent:
        copy.wait_send()


def on_device(dp_count, z_count, features, labels, embedding, weight_one, weight_two, cotangent):
    count = SAMPLES * dp_count * PLANES * z_count * Y_RING * CELLS
    dp_rows = PACKED // dp_count
    y_rows = dp_rows // Y_RING
    flat = (SAMPLES, CH, PLANES * DEPTH, SPAN)
    dma = pltpu.SemaphoreType.DMA
    field = pltpu.VMEM((SAMPLES, (PLANES + 2) * TRIPLE, PADDED), BF16)
    output, grad_one, grad_two = pl.pallas_call(
        functools.partial(body, dp_count, z_count, 1.0 / math.sqrt(count)),
        out_shape=(
            jax.ShapeDtypeStruct(flat, BF16),
            jax.ShapeDtypeStruct((27, CH, CH), F32),
            jax.ShapeDtypeStruct((27, CH, CH), F32),
        ),
        in_specs=[pl.BlockSpec(memory_space=pl.ANY)] * 6,
        out_specs=(
            pl.BlockSpec(memory_space=pl.ANY),
            pl.BlockSpec(memory_space=pltpu.VMEM),
            pl.BlockSpec(memory_space=pltpu.VMEM),
        ),
        scratch_shapes=[
            pltpu.VMEM(flat, BF16),
            pltpu.VMEM(flat, BF16),
            pltpu.VMEM((SAMPLES, PLANES, DEPTH, SPAN), jnp.int32),
            pltpu.VMEM((8, CH), F32),
            pltpu.VMEM((27, CH, CH), BF16),
            pltpu.VMEM((27, CH, CH), BF16),
            pltpu.VMEM((SAMPLES, CH * PLANES * DEPTH, SPAN), F32),
            field,
            field,
            field,
            pltpu.VMEM((SAMPLES, PLANES * TRIPLE, CELLS), BF16),
            pltpu.VMEM((SAMPLES, PLANES, CH, CELLS), F32),
            pltpu.VMEM((TRIPLE, PADDED), F32),
            pltpu.VMEM((TRIPLE, 3 * TRIPLE), BF16),
            pltpu.VMEM((TRIPLE, 3 * TRIPLE), BF16),
            pltpu.VMEM((TRIPLE, 3 * TRIPLE), BF16),
            pltpu.VMEM((9 * CH, TRIPLE), F32),
            pltpu.VMEM((2, PACKED, SPAN), BF16),
            pltpu.VMEM((2, dp_count - 1, dp_rows, SPAN), BF16),
            pltpu.VMEM((2, dp_rows, SPAN), BF16),
            pltpu.VMEM((2, Y_RING - 1, y_rows, SPAN), BF16),
            pltpu.VMEM((2, z_count, y_rows, SPAN), BF16),
            pltpu.VMEM((2, PACKED, SPAN), BF16),
            dma((8,)),
            dma((SAMPLES,)),
            dma((3, SAMPLES, 2)),
            dma((3, SAMPLES, 2)),
            dma((2, dp_count - 1)),
            dma((2, dp_count - 1)),
            dma((2, Y_RING - 1)),
            dma((2, Y_RING - 1)),
            dma((2, max(z_count - 1, 1))),
            dma((2, max(z_count - 1, 1))),
            dma((2, Y_RING - 1)),
            dma((2, Y_RING - 1)),
            dma((2, dp_count - 1)),
            dma((2, dp_count - 1)),
        ],
        compiler_params=pltpu.CompilerParams(
            collective_id=0, has_side_effects=True, vmem_limit_bytes=56 * 1024 * 1024
        ),
        name="surrogate",
    )(
        features.reshape(flat),
        labels,
        embedding,
        weight_one.reshape(27, CH, CH),
        weight_two.reshape(27, CH, CH),
        cotangent.reshape(flat),
    )
    taps = (3, 3, 3, CH, CH)
    return output.reshape(features.shape), grad_one.reshape(taps), grad_two.reshape(taps)


def solution(mesh):
    dp_count = mesh.shape["dp"]
    z_count = mesh.shape["gx"] // Y_RING
    placed = (
        P("dp", None, "gx", None, None),
        P("dp", "gx", None, None),
        P(),
        P(),
        P(),
        P("dp", None, "gx", None, None),
    )
    return jax.shard_map(
        functools.partial(on_device, dp_count, z_count),
        mesh=mesh,
        in_specs=placed,
        out_specs=(P("dp", None, "gx", None, None), P(), P()),
        check_vma=False,
    )
```

time: 427 us -> 70.2 us (0.16); the launches traced: 420 us -> 70 us
  waiting for transfers between devices: 259 us -> 0 us
  matrix products: 67.6 us -> 0 us
  Pallas kernels: 0 us -> 64.6 us
  local copies, waits for them, and re-layouts: 45.5 us -> 4.74 us
  starting transfers between devices: 18.7 us -> 0 us
  between operations: 15.4 us -> 0.65 us
  other arithmetic: 13.8 us -> 0 us
    psum x1 -> x0, waiting for transfers between devices: 253 us -> none  [on_device(): lax.psum((grad_first, grad_second), ('dp', 'gx'))]
    pallas_call x0 -> x1, Pallas kernels: none -> 64.6 us  [on_device(): pl.pallas_call(functools.partial(body, dp_count, z_count, 1.0 / math.sqrt...]
    conv_general_dilated x3 -> x0, matrix products: 35.9 us -> none  [convolve(): lax.conv_general_dilated(extended, kernel, (1, 1, 1), ((0, 0), (1, 1), (1...]
    dot_general x54 -> x0, matrix products: 31.7 us -> none  [tap_terms(): jnp.einsum('bixzy,boxzy->io', window, partner, preferred_element_type=jnp...]
    unnamed x101 -> x7, local copies, waits for them, and re-layouts: 27.5 us -> 4.74 us
    ppermute x6 -> x0, starting transfers between devices: 18.7 us -> none  [the longest x3 16.4 us: extended_2(): lax.ppermute(lax.slice_in_dim(block, 0, width, axis=dim), axis, backward)]
    convert_element_type x9 -> x0, local copies, waits for them, and re-layouts: 8.12 us -> none  [the longest x7 6.06 us: on_device(): hidden = jax.nn.silu(pre).astype(jnp.bfloat16)]
    ppermute x6 -> x0, waiting for transfers between devices: 6.26 us -> none  [the longest x3 6.25 us: extended_2(): lax.ppermute(lax.slice_in_dim(block, block.shape[dim] - width, None, axis...]
  transfers between devices with their start and end apart: 7 -> 0, of which waited for: 3 -> 0; matrix products, arithmetic and copies ran while one was open for 5% -> 0% of each run, Pallas kernels for 0% -> 0%
where the time goes in v1:
time: 70.2 us; the launch traced here: 70 us
  Pallas kernels  64.6 us (92%)
  local copies, waits for them, and re-layouts  4.74 us (7%)
    pallas_call x1, Pallas kernels, on_device(): pl.pallas_call(functools.partial(body, dp_count, z_count, 1.0 / math.sqrt...  64.6 us
    unnamed x7, local copies, waits for them, and re-layouts  4.74 us

profile of v1, /device:TPU:1, one launch (start us, length us, event | category | flops | bytes accessed | tf_op | source)
XLA Modules:
  0.0 70.0 jit_solution(11978966655642080370)
XLA Ops:
  0.6 64.6 %surrogate.1 = (bf16[2,64,32,128]{3,2,1,0:T(8,128)(2,1)}, f32[27,64,64]{2,1,0:T(8,128)}, f32[27,64,64]{2,1,0:T(8,128)}) custom-call(bf16[2,64,32,128]{3,2,1,0:T(8,128)(2,1)} %bitcast.7, s32[2,4,8,128]{3,2,1,0:T(8,128)} %labels_hbm.1, f32[8,64]{1,0:T(8,128)} %emb_hbm.1, bf16[27,64,64]{2,1,0:T(8,128)(2,1)} %bitcast.12, bf16[27,64,64]{2,1,0:T(8,128)(2,1)} %bitcast.13, ...), custom_call_target="tpu_custom_call" | custom-call | tf_op jit(solution)/shard_map/surrogate/pallas_call | solution.py:554
  65.3 0.0 copy-start.1
  65.3 2.3 %copy.12 = bf16[2,64,4,8,128]{4,3,2,1,0:T(8,128)(2,1)} copy(bf16[2,64,4,8,128]{4,3,2,1,0:T(8,128)(2,1)} %bitcast.9) | data formatting | bytes 2097152
  67.6 0.0 copy-done.1
  67.6 0.0 copy-start
  67.6 0.9 %copy.13 = f32[3,3,3,64,64]{4,3,2,1,0:T(8,128)} copy(f32[3,3,3,64,64]{4,3,2,1,0:T(8,128)S(1)} %bitcast.11) | data formatting | bytes 884736
  68.5 0.6 copy-done
  69.1 0.9 %copy.14 = f32[3,3,3,64,64]{4,3,2,1,0:T(8,128)} copy(f32[3,3,3,64,64]{4,3,2,1,0:T(8,128)S(1)} %bitcast.10) | data formatting | bytes 884736
Async XLA Ops:
  65.3 2.4 %copy-start.1 = (f32[27,64,64]{2,1,0:T(8,128)S(1)}, f32[27,64,64]{2,1,0:T(8,128)}, u32[]{:S(2)}) copy-start(f32[27,64,64]{2,1,0:T(8,128)} %get-tuple-element.7) | copy-start | bytes 1327108
  67.6 1.5 %copy-start = (f32[27,64,64]{2,1,0:T(8,128)S(1)}, f32[27,64,64]{2,1,0:T(8,128)}, u32[]{:S(2)}) copy-start(f32[27,64,64]{2,1,0:T(8,128)} %get-tuple-element.8) | copy-start | bytes 1327108

commit v2 on v1

--- a/solution.py
+++ b/solution.py
@@ -46,9 +46,8 @@
     one_hbm,
     two_hbm,
     cot_hbm,
-    out_hbm,
-    grad_one_ref,
-    grad_two_ref,
+    held,
+    full,
     feat,
     cot,
     labels,
@@ -71,9 +70,7 @@
     mine_y,
     got_y,
     all_z,
-    full,
     in_sem,
-    out_sem,
     halo_send,
     halo_recv,
     dp_send,
@@ -127,8 +124,9 @@
                 low = plane * TRIPLE + CH
                 field[s, low : low + CH, 0:SPAN] = jnp.zeros((CH, SPAN), BF16)
                 field[s, low : low + CH, PADDED - SPAN : PADDED] = jnp.zeros((CH, SPAN), BF16)
-    part[:, 0:SPAN] = jnp.zeros((TRIPLE, SPAN), F32)
-    part[:, PADDED - SPAN : PADDED] = jnp.zeros((TRIPLE, SPAN), F32)
+    for at in range(2):
+        part[at, :, 0:SPAN] = jnp.zeros((TRIPLE, SPAN), F32)
+        part[at, :, PADDED - SPAN : PADDED] = jnp.zeros((TRIPLE, SPAN), F32)
 
     barrier = pltpu.get_barrier_semaphore()
     peers = [left, right]
@@ -203,30 +201,23 @@
         return copies
 
     def halo_shifts(field, s, order):
-        def step(side, carry):
-            plane = side * (PLANES + 1)
+        for plane in (0, PLANES + 1):
+            low = plane * TRIPLE
+            own = field[s, low + CH : low + 2 * CH, SPAN : SPAN + CELLS].astype(F32)
             for z in range(DEPTH):
                 lanes = slice((z + 1) * SPAN, (z + 2) * SPAN)
-                value = field[s, rows(plane * TRIPLE + CH, CH), lanes].astype(F32)
-                before, after = shifted(value)
+                before, after = shifted(own[:, z * SPAN : (z + 1) * SPAN])
                 first, last = (after, before) if order > 0 else (before, after)
-                field[s, rows(plane * TRIPLE, CH), lanes] = first.astype(BF16)
-                field[s, rows(plane * TRIPLE + 2 * CH, CH), lanes] = last.astype(BF16)
-            return carry
-
-        lax.fori_loop(0, 2, step, 0)
+                field[s, low : low + CH, lanes] = first.astype(BF16)
+                field[s, low + 2 * CH : low + TRIPLE, lanes] = last.astype(BF16)
 
     halos = [[halo(field, which, s) for s in range(SAMPLES)] for which, field in enumerate((base3, cot3, hid3))]
 
     for s in range(SAMPLES):
         loads[2 + s].wait()
         widen(feat, s)
-
-        def plane_step(x, carry, s=s):
+        for x in range(PLANES):
             base_plane(s, x)
-            return carry
-
-        lax.fori_loop(0, PLANES, plane_step, 0)
         if s == 0:
             pl.semaphore_wait(barrier, len(peers))
         for copy in halos[0][s]:
@@ -234,12 +225,8 @@
     for s in range(SAMPLES):
         loads[4 + s].wait()
         widen(cot, s)
-
-        def plane_step(x, carry, s=s):
+        for x in range(PLANES):
             cot_plane(s, x)
-            return carry
-
-        lax.fori_loop(0, PLANES, plane_step, 0)
         for copy in halos[1][s]:
             copy.start()
 
@@ -267,93 +254,106 @@
             eye, flat, NT, preferred_element_type=F32
         ).astype(BF16)
 
-    def products(field, weights, s, x):
-        part[:, SPAN : SPAN + CELLS] = jnp.dot(
+    def products(field, weights, s, x, at):
+        part[at, :, SPAN : SPAN + CELLS] = jnp.dot(
             weights[...],
-            field[s, rows(x * TRIPLE, 3 * TRIPLE), SPAN : SPAN + CELLS],
+            field[s, x * TRIPLE : (x + 3) * TRIPLE, SPAN : SPAN + CELLS],
             preferred_element_type=F32,
         )
 
-    def summed(z, order):
-        total = part[CH : 2 * CH, (z + 1) * SPAN : (z + 2) * SPAN]
-        total = total + part[0:CH, (z + 1 - order) * SPAN : (z + 2 - order) * SPAN]
-        return total + part[2 * CH :, (z + 1 + order) * SPAN : (z + 2 + order) * SPAN]
-
-    def first_layer(s, x):
-        products(base3, w_one, s, x)
+    def summed(z, order, at):
+        total = part[at, CH : 2 * CH, (z + 1) * SPAN : (z + 2) * SPAN]
+        total = total + part[at, 0:CH, (z + 1 - order) * SPAN : (z + 2 - order) * SPAN]
+        return total + part[at, 2 * CH :, (z + 1 + order) * SPAN : (z + 2 + order) * SPAN]
+
+    def first_layer(s, x, at):
+        products(base3, w_one, s, x, at)
         for z in range(DEPTH):
-            pre = summed(z, 1)
+            pre = summed(z, 1, at)
             q = jax.nn.sigmoid(pre)
             factor[s, x, :, z * SPAN : (z + 1) * SPAN] = q * (1.0 + pre * (1.0 - q))
             put(hid3, s, x + 1, z, pre * q, 1)
 
-    def backward(s, x):
-        products(cot3, w_back, s, x)
+    def backward(s, x, at):
+        products(cot3, w_back, s, x, at)
         for z in range(DEPTH):
-            d_pre = summed(z, -1) * factor[s, x, :, z * SPAN : (z + 1) * SPAN]
+            d_pre = summed(z, -1, at) * factor[s, x, :, z * SPAN : (z + 1) * SPAN]
             before, after = shifted(d_pre)
             lanes = slice(z * SPAN, (z + 1) * SPAN)
             low = x * TRIPLE
-            dpre3[s, rows(low, CH), lanes] = before.astype(BF16)
-            dpre3[s, rows(low + CH, CH), lanes] = d_pre.astype(BF16)
-            dpre3[s, rows(low + 2 * CH, CH), lanes] = after.astype(BF16)
-
-    def second_layer(s, x):
-        products(hid3, w_two, s, x)
+            dpre3[s, low : low + CH, lanes] = before.astype(BF16)
+            dpre3[s, low + CH : low + 2 * CH, lanes] = d_pre.astype(BF16)
+            dpre3[s, low + 2 * CH : low + TRIPLE, lanes] = after.astype(BF16)
+
+    def second_layer(s, x, at):
+        products(hid3, w_two, s, x, at)
+        low = (x + 1) * TRIPLE + CH
         for z in range(DEPTH):
-            own = base3[s, rows((x + 1) * TRIPLE + CH, CH), (z + 1) * SPAN : (z + 2) * SPAN]
-            wide[s, pl.ds(x * DEPTH + z, CH, stride=PLANES * DEPTH), :] = summed(z, 1) + own.astype(F32)
-
-    def inner_planes(work):
-        def step(i, carry):
-            work(i // 2, 1 + i % 2)
-            return carry
-
-        lax.fori_loop(0, 4, step, 0)
-
-    def edge_planes(work, s):
-        def step(i, carry):
-            work(s, 3 * i)
-            return carry
-
-        lax.fori_loop(0, 2, step, 0)
-
-    inner_planes(first_layer)
+            own = base3[s, low : low + CH, (z + 1) * SPAN : (z + 2) * SPAN]
+            wide[s, pl.ds(x * DEPTH + z, CH, stride=PLANES * DEPTH), :] = summed(z, 1, at) + own.astype(F32)
+
+    def planes_of(work, places):
+        for i, (s, x) in enumerate(places):
+            work(s, x, i % 2)
+
+    inner = [(s, x) for s in range(SAMPLES) for x in range(1, PLANES - 1)]
+    edges = [(s, x) for s in range(SAMPLES) for x in (0, PLANES - 1)]
+
+    planes_of(first_layer, inner)
     for s in range(SAMPLES):
         for copy in halos[0][s]:
             copy.wait_recv()
+    for s in range(SAMPLES):
         halo_shifts(base3, s, 1)
-        edge_planes(first_layer, s)
+    planes_of(first_layer, edges)
+    for s in range(SAMPLES):
         for copy in halos[2][s]:
             copy.start()
-    inner_planes(backward)
+    planes_of(backward, inner)
     for s in range(SAMPLES):
         for copy in halos[1][s]:
             copy.wait_recv()
+    for s in range(SAMPLES):
         halo_shifts(cot3, s, -1)
-        edge_planes(backward, s)
+    planes_of(backward, edges)
 
     def gradient(g, field, partner, partner_plane, partner_lane):
         acc[...] = jnp.zeros_like(acc)
 
-        def step(i, carry):
-            s = i // PLANES
-            x = i % PLANES
+        def step(s, carry):
             taps = jnp.concatenate(
                 [
-                    field[s, rows((x + a) * TRIPLE + CH, CH), b * SPAN : b * SPAN + CELLS]
+                    jnp.concatenate(
+                        [
+                            field[
+                                s,
+                                (x + a) * TRIPLE + CH : (x + a) * TRIPLE + 2 * CH,
+                                b * SPAN : b * SPAN + CELLS,
+                            ]
+                            for x in range(PLANES)
+                        ],
+                        axis=1,
+                    )
                     for a in range(3)
                     for b in range(3)
                 ],
                 axis=0,
             )
-            other = partner[
-                s, rows((x + partner_plane) * TRIPLE, TRIPLE), partner_lane : partner_lane + CELLS
-            ]
+            other = jnp.concatenate(
+                [
+                    partner[
+                        s,
+                        (x + partner_plane) * TRIPLE : (x + partner_plane + 1) * TRIPLE,
+                        partner_lane : partner_lane + CELLS,
+                    ]
+                    for x in range(PLANES)
+                ],
+                axis=1,
+            )
             acc[...] += lax.dot_general(taps, other, NT, preferred_element_type=F32)
             return carry
 
-        lax.fori_loop(0, SAMPLES * PLANES, step, 0)
+        lax.fori_loop(0, SAMPLES, step, 0)
         half = 9 * CH // 2
         packed[g, 0 : 9 * CH, :] = acc[:, 0:SPAN].astype(BF16)
         packed[g, 9 * CH : 9 * CH + half, :] = jnp.concatenate(
@@ -475,21 +475,6 @@
         arrived(yg_copies)
         return start(gather_dp(g))
 
-    def stage_five(g, dg_copies, target):
-        arrived(dg_copies)
-        half = 9 * CH // 2
-        for tap in range(9):
-            block = full[g, tap * CH : (tap + 1) * CH, :].astype(F32)
-            target[tap * 3] = block[:, 0:CH]
-            target[tap * 3 + 1] = block[:, CH:]
-        for piece in range(18):
-            low = piece * 32
-            lane = 0
-            if low >= half:
-                low, lane = low - half, CH
-            block = full[g, 9 * CH + low : 9 * CH + low + 32, lane : lane + CH].astype(F32)
-            target[(piece // 2) * 3 + 2, (piece % 2) * 32 : (piece % 2) * 32 + 32, :] = block
-
     gradient(0, base3, dpre3, 0, 0)
     wait_zero = start(sum_dp(0))
     for s in range(SAMPLES):
@@ -500,48 +485,56 @@
     wait_one = start(sum_dp(1))
     wait_zero = stage_one(0, wait_zero)
 
-    def two_planes(s, first):
-        def step(i, carry):
-            second_layer(s, first + i)
-            return carry
-
-        lax.fori_loop(0, 2, step, 0)
-
     def give_back(s):
         def step(c, carry):
             block = wide[s, rows(c * 8 * PLANES * DEPTH, 8 * PLANES * DEPTH), :]
-            feat[s, pl.ds(c * 8, 8)] = block.reshape(8, PLANES * DEPTH, SPAN).astype(BF16)
+            held[s, pl.ds(c * 8, 8)] = block.reshape(8, PLANES * DEPTH, SPAN).astype(BF16)
             return carry
 
         lax.fori_loop(0, CH // 8, step, 0)
-        copy = pltpu.make_async_copy(feat.at[s], out_hbm.at[s], out_sem.at[s])
-        copy.start()
-        return copy
-
-    two_planes(0, 0)
+
+    planes_of(second_layer, [(0, x) for x in range(PLANES)])
     wait_one = stage_one(1, wait_one)
     wait_zero = stage_two(0, wait_zero)
-    two_planes(0, 2)
+    give_back(0)
+    planes_of(second_layer, [(1, x) for x in range(PLANES)])
     wait_one = stage_two(1, wait_one)
     wait_zero = stage_three(0, wait_zero)
-    out_zero = give_back(0)
-    two_planes(1, 0)
+    give_back(1)
     wait_one = stage_three(1, wait_one)
     wait_zero = stage_four(0, wait_zero)
-    two_planes(1, 2)
     wait_one = stage_four(1, wait_one)
-    out_one = give_back(1)
-    stage_five(0, wait_zero, grad_one_ref)
-    stage_five(1, wait_one, grad_two_ref)
-
-    out_zero.wait()
-    out_one.wait()
+    arrived(wait_zero)
+    arrived(wait_one)
+
     for field in halos:
         for side in field:
             for copy in side:
                 copy.wait_send()
     for copy in sent:
         copy.wait_send()
+
+
+def finish(held, sums, out_hbm, grad_one, grad_two, spread, sems):
+    copies = [pltpu.make_async_copy(held, out_hbm, sems.at[0])]
+    copies[0].start()
+    half = 9 * CH // 2
+    for g, target in enumerate((grad_one, grad_two)):
+        for tap in range(9):
+            block = sums[g, tap * CH : (tap + 1) * CH, :].astype(F32)
+            spread[g, tap * 3] = block[:, 0:CH]
+            spread[g, tap * 3 + 1] = block[:, CH:]
+        for piece in range(18):
+            low = piece * 32
+            lane = 0
+            if low >= half:
+                low, lane = low - half, CH
+            block = sums[g, 9 * CH + low : 9 * CH + low + 32, lane : lane + CH].astype(F32)
+            spread[g, (piece // 2) * 3 + 2, (piece % 2) * 32 : (piece % 2) * 32 + 32, :] = block
+        copies.append(pltpu.make_async_copy(spread.at[g], target, sems.at[1 + g]))
+        copies[-1].start()
+    for copy in copies:
+        copy.wait()
 
 
 def on_device(dp_count, z_count, features, labels, embedding, weight_one, weight_two, cotangent):
@@ -551,19 +544,11 @@
     flat = (SAMPLES, CH, PLANES * DEPTH, SPAN)
     dma = pltpu.SemaphoreType.DMA
     field = pltpu.VMEM((SAMPLES, (PLANES + 2) * TRIPLE, PADDED), BF16)
-    output, grad_one, grad_two = pl.pallas_call(
+    held, sums = pl.pallas_call(
         functools.partial(body, dp_count, z_count, 1.0 / math.sqrt(count)),
-        out_shape=(
-            jax.ShapeDtypeStruct(flat, BF16),
-            jax.ShapeDtypeStruct((27, CH, CH), F32),
-            jax.ShapeDtypeStruct((27, CH, CH), F32),
-        ),
-        in_specs=[pl.BlockSpec(memory_space=pl.ANY)] * 6,
-        out_specs=(
-            pl.BlockSpec(memory_space=pl.ANY),
-            pl.BlockSpec(memory_space=pltpu.VMEM),
-            pl.BlockSpec(memory_space=pltpu.VMEM),
-        ),
+        out_shape=(pltpu.VMEM(flat, BF16), pltpu.VMEM((2, PACKED, SPAN), BF16)),
+        in_specs=[pl.BlockSpec(memory_space=pltpu.HBM)] * 6,
+        out_specs=(pl.BlockSpec(memory_space=pltpu.VMEM),) * 2,
         scratch_shapes=[
             pltpu.VMEM(flat, BF16),
             pltpu.VMEM(flat, BF16),
@@ -577,7 +562,7 @@
             field,
             pltpu.VMEM((SAMPLES, PLANES * TRIPLE, CELLS), BF16),
             pltpu.VMEM((SAMPLES, PLANES, CH, CELLS), F32),
-            pltpu.VMEM((TRIPLE, PADDED), F32),
+            pltpu.VMEM((2, TRIPLE, PADDED), F32),
             pltpu.VMEM((TRIPLE, 3 * TRIPLE), BF16),
             pltpu.VMEM((TRIPLE, 3 * TRIPLE), BF16),
             pltpu.VMEM((TRIPLE, 3 * TRIPLE), BF16),
@@ -587,9 +572,7 @@
             pltpu.VMEM((2, dp_rows, SPAN), BF16),
             pltpu.VMEM((2, Y_RING - 1, y_rows, SPAN), BF16),
             pltpu.VMEM((2, z_count, y_rows, SPAN), BF16),
-            pltpu.VMEM((2, PACKED, SPAN), BF16),
             dma((8,)),
-            dma((SAMPLES,)),
             dma((3, SAMPLES, 2)),
             dma((3, SAMPLES, 2)),
             dma((2, dp_count - 1)),
@@ -615,6 +598,19 @@
         weight_two.reshape(27, CH, CH),
         cotangent.reshape(flat),
     )
+    output, grad_one, grad_two = pl.pallas_call(
+        finish,
+        out_shape=(
+            jax.ShapeDtypeStruct(flat, BF16),
+            jax.ShapeDtypeStruct((27, CH, CH), F32),
+            jax.ShapeDtypeStruct((27, CH, CH), F32),
+        ),
+        in_specs=[pl.BlockSpec(memory_space=pltpu.VMEM)] * 2,
+        out_specs=(pl.BlockSpec(memory_space=pltpu.HBM),) * 3,
+        scratch_shapes=[pltpu.VMEM((2, 27, CH, CH), F32), dma((3,))],
+        compiler_params=pltpu.CompilerParams(vmem_limit_bytes=16 * 1024 * 1024),
+        name="finish",
+    )(held, sums)
     taps = (3, 3, 3, CH, CH)
     return output.reshape(features.shape), grad_one.reshape(taps), grad_two.reshape(taps)
 

time: 70.2 us -> 58.9 us (0.84)
  Pallas kernels: 64.6 us -> 58 us
  local copies, waits for them, and re-layouts: 4.74 us -> 0 us
    pallas_call x1, Pallas kernels: 64.6 us -> 56.5 us  [on_device(): pl.pallas_call(functools.partial(body, dp_count, z_count, 1.0 / math.sqrt...]
    unnamed x7 -> x0, local copies, waits for them, and re-layouts: 4.74 us -> none
    pallas_call x0 -> x1, Pallas kernels: none -> 1.58 us  [on_device(): pl.pallas_call(finish, out_shape=(jax.ShapeDtypeStruct(flat, BF16), jax.S...]
where the time goes in v2:
time: 58.9 us; the launch traced here: 58.8 us
  Pallas kernels  58 us (98%)
  between operations  0.8 us (1%)
    pallas_call x1, Pallas kernels, on_device(): pl.pallas_call(functools.partial(body, dp_count, z_count, 1.0 / math.sqrt...  56.5 us
    pallas_call x1, Pallas kernels, on_device(): pl.pallas_call(finish, out_shape=(jax.ShapeDtypeStruct(flat, BF16), jax.S...  1.58 us

profile of v2, /device:TPU:1, one launch (start us, length us, event | category | flops | bytes accessed | tf_op | source)
XLA Modules:
  0.0 58.8 jit_solution(8742366552986341134)
XLA Ops:
  0.6 56.5 %surrogate.1 = (bf16[2,64,32,128]{3,2,1,0:T(8,128)(2,1)S(1)}, bf16[2,1024,128]{2,1,0:T(8,128)(2,1)S(1)}) custom-call(bf16[2,64,32,128]{3,2,1,0:T(8,128)(2,1)} %bitcast.7, s32[2,4,8,128]{3,2,1,0:T(8,128)} %labels_hbm.1, f32[8,64]{1,0:T(8,128)} %emb_hbm.1, bf16[27,64,64]{2,1,0:T(8,128)(2,1)} %bitcast.9, bf16[27,64,64]{2,1,0:T(8,128)(2,1)} %bitcast.10, ...), custom_call_target="tpu_custom_call" | custom-call | tf_op jit(solution)/shard_map/surrogate/pallas_call | solution.py:547
  57.1 1.6 %finish.1 = (bf16[2,64,32,128]{3,2,1,0:T(8,128)(2,1)}, f32[27,64,64]{2,1,0:T(8,128)}, f32[27,64,64]{2,1,0:T(8,128)}) custom-call(bf16[2,64,32,128]{3,2,1,0:T(8,128)(2,1)S(1)} %get-tuple-element.8.held, bf16[2,1024,128]{2,1,0:T(8,128)(2,1)S(1)} %get-tuple-element.9.sums), custom_call_target="tpu_custom_call" | custom-call | tf_op jit(solution)/shard_map/finish/pallas_call | solution.py:601

commit v3 on v2

--- a/solution.py
+++ b/solution.py
@@ -66,24 +66,16 @@
     w_back,
     acc,
     packed,
-    got_dp,
-    mine_y,
-    got_y,
+    got_core,
+    mine,
+    got_xy,
     all_z,
     in_sem,
     halo_send,
     halo_recv,
-    dp_send,
-    dp_recv,
-    y_send,
-    y_recv,
-    z_send,
-    z_recv,
-    yg_send,
-    yg_recv,
-    dg_send,
-    dg_recv,
+    *links,
 ):
+    sum_core, sum_xy, sum_z, back_xy, back_core = zip(links[0::2], links[1::2])
     me_dp = lax.axis_index("dp")
     me_gx = lax.axis_index("gx")
     gx_count = z_count * Y_RING
@@ -92,11 +84,16 @@
     left = (me_dp, (me_gx + gx_count - 1) % gx_count)
     right = (me_dp, (me_gx + 1) % gx_count)
 
-    def dp_peer(k):
-        return ((me_dp + k) % dp_count, me_gx)
-
-    def y_peer(k):
-        return (me_dp, me_z * Y_RING + (me_y + k) % Y_RING)
+    x_count = dp_count // 2
+    me_x = me_dp // 2
+    me_core = me_dp % 2
+    xy_count = x_count * Y_RING
+    me_xy = me_x * Y_RING + me_y
+    sibling = (me_x * 2 + 1 - me_core, me_gx)
+
+    def xy_peer(k):
+        to = (me_xy + k) % xy_count
+        return ((to // Y_RING) * 2 + me_core, me_z * Y_RING + to % Y_RING)
 
     def z_peer(k):
         return (me_dp, ((me_z + k) % z_count) * Y_RING + me_y)
@@ -118,7 +115,7 @@
         copy.start()
         loads.append(copy)
 
-    for field in (base3, hid3):
+    for field in (base3, cot3):
         for s in range(SAMPLES):
             for plane in range(PLANES + 2):
                 low = plane * TRIPLE + CH
@@ -129,9 +126,8 @@
         part[at, :, PADDED - SPAN : PADDED] = jnp.zeros((TRIPLE, SPAN), F32)
 
     barrier = pltpu.get_barrier_semaphore()
-    peers = [left, right]
-    peers += [dp_peer(k) for k in range(1, dp_count)]
-    peers += [y_peer(k) for k in range(1, Y_RING)]
+    peers = [left, right, sibling]
+    peers += [xy_peer(k) for k in range(1, xy_count)]
     peers += [z_peer(k) for k in range(1, z_count)]
     for peer in peers:
         pl.semaphore_signal(barrier, inc=1, device_id=peer, device_id_type=MESH)
@@ -299,141 +295,54 @@
     inner = [(s, x) for s in range(SAMPLES) for x in range(1, PLANES - 1)]
     edges = [(s, x) for s in range(SAMPLES) for x in (0, PLANES - 1)]
 
-    planes_of(first_layer, inner)
-    for s in range(SAMPLES):
-        for copy in halos[0][s]:
-            copy.wait_recv()
-    for s in range(SAMPLES):
-        halo_shifts(base3, s, 1)
-    planes_of(first_layer, edges)
-    for s in range(SAMPLES):
-        for copy in halos[2][s]:
-            copy.start()
-    planes_of(backward, inner)
-    for s in range(SAMPLES):
-        for copy in halos[1][s]:
-            copy.wait_recv()
-    for s in range(SAMPLES):
-        halo_shifts(cot3, s, -1)
-    planes_of(backward, edges)
-
-    def gradient(g, field, partner, partner_plane, partner_lane):
-        acc[...] = jnp.zeros_like(acc)
-
-        def step(s, carry):
-            taps = jnp.concatenate(
-                [
-                    jnp.concatenate(
-                        [
-                            field[
-                                s,
-                                (x + a) * TRIPLE + CH : (x + a) * TRIPLE + 2 * CH,
-                                b * SPAN : b * SPAN + CELLS,
-                            ]
-                            for x in range(PLANES)
-                        ],
-                        axis=1,
-                    )
-                    for a in range(3)
-                    for b in range(3)
-                ],
-                axis=0,
-            )
-            other = jnp.concatenate(
-                [
-                    partner[
-                        s,
-                        (x + partner_plane) * TRIPLE : (x + partner_plane + 1) * TRIPLE,
-                        partner_lane : partner_lane + CELLS,
-                    ]
-                    for x in range(PLANES)
-                ],
-                axis=1,
-            )
-            acc[...] += lax.dot_general(taps, other, NT, preferred_element_type=F32)
-            return carry
-
-        lax.fori_loop(0, SAMPLES, step, 0)
-        half = 9 * CH // 2
-        packed[g, 0 : 9 * CH, :] = acc[:, 0:SPAN].astype(BF16)
-        packed[g, 9 * CH : 9 * CH + half, :] = jnp.concatenate(
-            [acc[0:half, SPAN:TRIPLE], acc[half : 2 * half, SPAN:TRIPLE]], axis=1
-        ).astype(BF16)
-        packed[g, 9 * CH + half :, :] = jnp.zeros((PACKED - 9 * CH - half, SPAN), BF16)
-
-    dp_rows = PACKED // dp_count
-    y_rows = dp_rows // Y_RING
-
-    def sum_dp(g):
-        return [
-            pltpu.make_async_remote_copy(
-                src_ref=packed.at[g, rows(((me_dp + k) % dp_count) * dp_rows, dp_rows)],
-                dst_ref=got_dp.at[g, k - 1],
-                send_sem=dp_send.at[g, k - 1],
-                recv_sem=dp_recv.at[g, k - 1],
-                device_id=dp_peer(k),
-                device_id_type=MESH,
-            )
-            for k in range(1, dp_count)
-        ]
-
-    def sum_y(g):
-        return [
-            pltpu.make_async_remote_copy(
-                src_ref=mine_y.at[g, rows(((me_y + k) % Y_RING) * y_rows, y_rows)],
-                dst_ref=got_y.at[g, k - 1],
-                send_sem=y_send.at[g, k - 1],
-                recv_sem=y_recv.at[g, k - 1],
-                device_id=y_peer(k),
-                device_id_type=MESH,
-            )
-            for k in range(1, Y_RING)
-        ]
-
-    def spread_z(g):
-        return [
-            pltpu.make_async_remote_copy(
-                src_ref=all_z.at[g, me_z],
-                dst_ref=all_z.at[g, me_z],
-                send_sem=z_send.at[g, k - 1],
-                recv_sem=z_recv.at[g, k - 1],
-                device_id=z_peer(k),
-                device_id_type=MESH,
-            )
-            for k in range(1, z_count)
-        ]
-
-    def my_y_rows():
-        return rows(me_dp * dp_rows + me_y * y_rows, y_rows)
-
-    def my_dp_rows():
-        return rows(me_dp * dp_rows, dp_rows)
-
-    def gather_y(g):
-        return [
-            pltpu.make_async_remote_copy(
-                src_ref=full.at[g, my_y_rows()],
-                dst_ref=full.at[g, my_y_rows()],
-                send_sem=yg_send.at[g, k - 1],
-                recv_sem=yg_recv.at[g, k - 1],
-                device_id=y_peer(k),
-                device_id_type=MESH,
-            )
-            for k in range(1, Y_RING)
-        ]
-
-    def gather_dp(g):
-        return [
-            pltpu.make_async_remote_copy(
-                src_ref=full.at[g, my_dp_rows()],
-                dst_ref=full.at[g, my_dp_rows()],
-                send_sem=dg_send.at[g, k - 1],
-                recv_sem=dg_recv.at[g, k - 1],
-                device_id=dp_peer(k),
-                device_id_type=MESH,
-            )
-            for k in range(1, dp_count)
-        ]
+    def gradient(total, taps_of, others_of, places):
+        taps = jnp.concatenate(
+            [
+                jnp.concatenate([taps_of(s, x, a, b) for s, x in places], axis=1)
+                for a in range(3)
+                for b in range(3)
+            ],
+            axis=0,
+        )
+        others = jnp.concatenate([others_of(s, x) for s, x in places], axis=1)
+        return total + lax.dot_general(taps, others, NT, preferred_element_type=F32)
+
+    def base_taps(s, x, a, b):
+        low = (x + a) * TRIPLE + CH
+        return base3[s, low : low + CH, b * SPAN : b * SPAN + CELLS]
+
+    def d_pre_of(s, x):
+        return dpre3[s, x * TRIPLE : (x + 1) * TRIPLE, :]
+
+    def cot_taps(s, x, a, b):
+        low = (x + 2 - a) * TRIPLE + CH
+        return cot3[s, low : low + CH, (2 - b) * SPAN : (2 - b) * SPAN + CELLS]
+
+    def hidden_of(s, x):
+        return hid3[s, (x + 1) * TRIPLE : (x + 2) * TRIPLE, SPAN : SPAN + CELLS]
+
+    def pack(g, total):
+        packed[g, 0 : 9 * CH, :] = total[:, 0:SPAN].astype(BF16)
+        last = total[:, SPAN:TRIPLE]
+        for pair in range(5):
+            one_tap = last[2 * pair * CH : (2 * pair + 1) * CH]
+            next_tap = last[(2 * pair + 1) * CH : (2 * pair + 2) * CH] if pair < 4 else jnp.zeros_like(one_tap)
+            low = (9 + pair) * CH
+            packed[g, low : low + CH, :] = jnp.concatenate([one_tap, next_tap], axis=1).astype(BF16)
+        packed[g, 14 * CH :, :] = jnp.zeros((PACKED - 14 * CH, SPAN), BF16)
+
+    half = PACKED // 2
+    chunk = half // xy_count
+
+    def remote(src, dst, sems, at, peer):
+        return pltpu.make_async_remote_copy(
+            src_ref=src,
+            dst_ref=dst,
+            send_sem=sems[0].at[at],
+            recv_sem=sems[1].at[at],
+            device_id=peer,
+            device_id_type=MESH,
+        )
 
     sent = []
 
@@ -447,43 +356,49 @@
         for copy in copies:
             copy.wait_recv()
 
-    def stage_one(g, dp_copies):
-        arrived(dp_copies)
-        total = packed[g, my_dp_rows(), :].astype(F32)
-        for k in range(dp_count - 1):
-            total = total + got_dp[g, k].astype(F32)
-        mine_y[g] = total.astype(BF16)
-        return start(sum_y(g))
-
-    def stage_two(g, y_copies):
-        arrived(y_copies)
-        total = mine_y[g, rows(me_y * y_rows, y_rows), :].astype(F32)
-        for k in range(Y_RING - 1):
-            total = total + got_y[g, k].astype(F32)
-        all_z[g, me_z] = total.astype(BF16)
-        return start(spread_z(g))
-
-    def stage_three(g, z_copies):
-        arrived(z_copies)
-        total = all_z[g, 0].astype(F32)
+    def my_half():
+        return rows(me_core * half, half)
+
+    def my_chunk():
+        return rows(me_core * half + me_xy * chunk, chunk)
+
+    def to_sibling(g):
+        src = packed.at[g, rows((1 - me_core) * half, half)]
+        return start([remote(src, got_core.at[g], sum_core, g, sibling)])
+
+    def spread_xy(g, copies):
+        arrived(copies)
+        total = packed[g, my_half(), :].astype(F32) + got_core[g].astype(F32)
+        mine[g] = total.astype(BF16)
+        copies = []
+        for k in range(1, xy_count):
+            src = mine.at[g, rows(((me_xy + k) % xy_count) * chunk, chunk)]
+            copies.append(remote(src, got_xy.at[g, k - 1], sum_xy, (g, k - 1), xy_peer(k)))
+        return start(copies)
+
+    def spread_z(waits):
+        for g, copies in enumerate(waits):
+            arrived(copies)
+            total = mine[g, rows(me_xy * chunk, chunk), :].astype(F32)
+            for k in range(xy_count - 1):
+                total = total + got_xy[g, k].astype(F32)
+            all_z[me_z, g] = total.astype(BF16)
+        own = all_z.at[me_z]
+        return start([remote(own, own, sum_z, k - 1, z_peer(k)) for k in range(1, z_count)])
+
+    def gather_xy(copies):
+        arrived(copies)
+        total = all_z[0].astype(F32)
         for k in range(1, z_count):
-            total = total + all_z[g, k].astype(F32)
-        full[g, my_y_rows(), :] = (total * scale).astype(BF16)
-        return start(gather_y(g))
-
-    def stage_four(g, yg_copies):
-        arrived(yg_copies)
-        return start(gather_dp(g))
-
-    gradient(0, base3, dpre3, 0, 0)
-    wait_zero = start(sum_dp(0))
-    for s in range(SAMPLES):
-        for copy in halos[2][s]:
-            copy.wait_recv()
-        halo_shifts(hid3, s, 1)
-    gradient(1, hid3, cot3, 1, SPAN)
-    wait_one = start(sum_dp(1))
-    wait_zero = stage_one(0, wait_zero)
+            total = total + all_z[k].astype(F32)
+        full[:, my_chunk(), :] = (total * scale).astype(BF16)
+        own = full.at[:, my_chunk()]
+        return start([remote(own, own, back_xy, k - 1, xy_peer(k)) for k in range(1, xy_count)])
+
+    def gather_core(copies):
+        arrived(copies)
+        own = full.at[:, my_half()]
+        return start([remote(own, own, back_core, 0, sibling)])
 
     def give_back(s):
         def step(c, carry):
@@ -493,19 +408,44 @@
 
         lax.fori_loop(0, CH // 8, step, 0)
 
-    planes_of(second_layer, [(0, x) for x in range(PLANES)])
-    wait_one = stage_one(1, wait_one)
-    wait_zero = stage_two(0, wait_zero)
+    planes_of(first_layer, inner)
+    planes_of(backward, inner)
+    acc[1] = gradient(0.0, cot_taps, hidden_of, inner)
+    for s in range(SAMPLES):
+        for copy in halos[0][s]:
+            copy.wait_recv()
+    for s in range(SAMPLES):
+        halo_shifts(base3, s, 1)
+    planes_of(first_layer, edges)
+    for s in range(SAMPLES):
+        for copy in halos[2][s]:
+            copy.start()
+    acc[0] = gradient(0.0, base_taps, d_pre_of, inner)
+    for s in range(SAMPLES):
+        for copy in halos[1][s]:
+            copy.wait_recv()
+    for s in range(SAMPLES):
+        halo_shifts(cot3, s, -1)
+    planes_of(backward, edges)
+    pack(0, gradient(acc[0], base_taps, d_pre_of, edges))
+    core_zero = to_sibling(0)
+    pack(1, gradient(acc[1], cot_taps, hidden_of, edges))
+    core_one = to_sibling(1)
+    xy_zero = spread_xy(0, core_zero)
+    planes_of(second_layer, inner)
+    xy_one = spread_xy(1, core_one)
+    for s in range(SAMPLES):
+        for copy in halos[2][s]:
+            copy.wait_recv()
+    for s in range(SAMPLES):
+        halo_shifts(hid3, s, 1)
+    planes_of(second_layer, edges)
+    waits = spread_z((xy_zero, xy_one))
     give_back(0)
-    planes_of(second_layer, [(1, x) for x in range(PLANES)])
-    wait_one = stage_two(1, wait_one)
-    wait_zero = stage_three(0, wait_zero)
     give_back(1)
-    wait_one = stage_three(1, wait_one)
-    wait_zero = stage_four(0, wait_zero)
-    wait_one = stage_four(1, wait_one)
-    arrived(wait_zero)
-    arrived(wait_one)
+    waits = gather_xy(waits)
+    waits = gather_core(waits)
+    arrived(waits)
 
     for field in halos:
         for side in field:
@@ -518,19 +458,27 @@
 def finish(held, sums, out_hbm, grad_one, grad_two, spread, sems):
     copies = [pltpu.make_async_copy(held, out_hbm, sems.at[0])]
     copies[0].start()
-    half = 9 * CH // 2
+    eye = (
+        lax.broadcasted_iota(jnp.int32, (SPAN, SPAN), 0)
+        == lax.broadcasted_iota(jnp.int32, (SPAN, SPAN), 1)
+    ).astype(BF16)
     for g, target in enumerate((grad_one, grad_two)):
-        for tap in range(9):
-            block = sums[g, tap * CH : (tap + 1) * CH, :].astype(F32)
-            spread[g, tap * 3] = block[:, 0:CH]
-            spread[g, tap * 3 + 1] = block[:, CH:]
-        for piece in range(18):
-            low = piece * 32
-            lane = 0
-            if low >= half:
-                low, lane = low - half, CH
-            block = sums[g, 9 * CH + low : 9 * CH + low + 32, lane : lane + CH].astype(F32)
-            spread[g, (piece // 2) * 3 + 2, (piece % 2) * 32 : (piece % 2) * 32 + 32, :] = block
+        for piece in range(14):
+            block = sums[g, piece * CH : (piece + 1) * CH, :]
+            if g == 0:
+                block = block.astype(F32)
+                pair = (block[:, 0:CH], block[:, CH:])
+            else:
+                block = lax.dot_general(eye, block, NT, preferred_element_type=F32)
+                pair = (block[0:CH], block[CH:])
+            if piece < 9:
+                spread[g, piece * 3] = pair[0]
+                spread[g, piece * 3 + 1] = pair[1]
+            else:
+                tap = 2 * (piece - 9)
+                spread[g, tap * 3 + 2] = pair[0]
+                if tap < 8:
+                    spread[g, tap * 3 + 5] = pair[1]
         copies.append(pltpu.make_async_copy(spread.at[g], target, sems.at[1 + g]))
         copies[-1].start()
     for copy in copies:
@@ -539,8 +487,9 @@
 
 def on_device(dp_count, z_count, features, labels, embedding, weight_one, weight_two, cotangent):
     count = SAMPLES * dp_count * PLANES * z_count * Y_RING * CELLS
-    dp_rows = PACKED // dp_count
-    y_rows = dp_rows // Y_RING
+    half = PACKED // 2
+    xy_count = dp_count // 2 * Y_RING
+    chunk = half // xy_count
     flat = (SAMPLES, CH, PLANES * DEPTH, SPAN)
     dma = pltpu.SemaphoreType.DMA
     field = pltpu.VMEM((SAMPLES, (PLANES + 2) * TRIPLE, PADDED), BF16)
@@ -566,25 +515,20 @@
             pltpu.VMEM((TRIPLE, 3 * TRIPLE), BF16),
             pltpu.VMEM((TRIPLE, 3 * TRIPLE), BF16),
             pltpu.VMEM((TRIPLE, 3 * TRIPLE), BF16),
-            pltpu.VMEM((9 * CH, TRIPLE), F32),
+            pltpu.VMEM((2, 9 * CH, TRIPLE), F32),
             pltpu.VMEM((2, PACKED, SPAN), BF16),
-            pltpu.VMEM((2, dp_count - 1, dp_rows, SPAN), BF16),
-            pltpu.VMEM((2, dp_rows, SPAN), BF16),
-            pltpu.VMEM((2, Y_RING - 1, y_rows, SPAN), BF16),
-            pltpu.VMEM((2, z_count, y_rows, SPAN), BF16),
+            pltpu.VMEM((2, half, SPAN), BF16),
+            pltpu.VMEM((2, half, SPAN), BF16),
+            pltpu.VMEM((2, xy_count - 1, chunk, SPAN), BF16),
+            pltpu.VMEM((z_count, 2, chunk, SPAN), BF16),
             dma((8,)),
             dma((3, SAMPLES, 2)),
             dma((3, SAMPLES, 2)),
-            dma((2, dp_count - 1)),
-            dma((2, dp_count - 1)),
-            dma((2, Y_RING - 1)),
-            dma((2, Y_RING - 1)),
-            dma((2, max(z_count - 1, 1))),
-            dma((2, max(z_count - 1, 1))),
-            dma((2, Y_RING - 1)),
-            dma((2, Y_RING - 1)),
-            dma((2, dp_count - 1)),
-            dma((2, dp_count - 1)),
+        ]
+        + [
+            dma(shape)
+            for shape in ((2,), (2, xy_count - 1), (max(z_count - 1, 1),), (xy_count - 1,), (1,))
+            for _ in range(2)
         ],
         compiler_params=pltpu.CompilerParams(
             collective_id=0, has_side_effects=True, vmem_limit_bytes=56 * 1024 * 1024

time: 58.9 us -> 56.5 us (0.959)
  Pallas kernels: 58 us -> 55.6 us
    pallas_call x1, Pallas kernels: 56.5 us -> 54 us  [on_device(): pl.pallas_call(functools.partial(body, dp_count, z_count, 1.0 / math.sqrt...]
where the time goes in v3:
time: 56.5 us; the launch traced here: 56.4 us
  Pallas kernels  55.6 us (98%)
  between operations  0.82 us (1%)
    pallas_call x1, Pallas kernels, on_device(): pl.pallas_call(functools.partial(body, dp_count, z_count, 1.0 / math.sqrt...  54 us
    pallas_call x1, Pallas kernels, on_device(): pl.pallas_call(finish, out_shape=(jax.ShapeDtypeStruct(flat, BF16), jax.S...  1.58 us

profile of v3, /device:TPU:1, one launch (start us, length us, event | category | flops | bytes accessed | tf_op | source)
XLA Modules:
  0.0 56.4 jit_solution(4067424939589049990)
XLA Ops:
  0.6 54.0 %surrogate.1 = (bf16[2,64,32,128]{3,2,1,0:T(8,128)(2,1)S(1)}, bf16[2,1024,128]{2,1,0:T(8,128)(2,1)S(1)}) custom-call(bf16[2,64,32,128]{3,2,1,0:T(8,128)(2,1)} %bitcast.7, s32[2,4,8,128]{3,2,1,0:T(8,128)} %labels_hbm.1, f32[8,64]{1,0:T(8,128)} %emb_hbm.1, bf16[27,64,64]{2,1,0:T(8,128)(2,1)} %bitcast.9, bf16[27,64,64]{2,1,0:T(8,128)(2,1)} %bitcast.10, ...), custom_call_target="tpu_custom_call" | custom-call | tf_op jit(solution)/shard_map/surrogate/pallas_call | solution.py:496
  54.6 1.6 %finish.1 = (bf16[2,64,32,128]{3,2,1,0:T(8,128)(2,1)}, f32[27,64,64]{2,1,0:T(8,128)}, f32[27,64,64]{2,1,0:T(8,128)}) custom-call(bf16[2,64,32,128]{3,2,1,0:T(8,128)(2,1)S(1)} %get-tuple-element.8.held, bf16[2,1024,128]{2,1,0:T(8,128)(2,1)S(1)} %get-tuple-element.9.sums), custom_call_target="tpu_custom_call" | custom-call | tf_op jit(solution)/shard_map/finish/pallas_call | solution.py:545

commit v4 on v3

--- a/solution.py
+++ b/solution.py
@@ -64,6 +64,7 @@
     w_one,
     w_two,
     w_back,
+    w_tail,
     acc,
     packed,
     got_core,
@@ -91,9 +92,25 @@
     me_xy = me_x * Y_RING + me_y
     sibling = (me_x * 2 + 1 - me_core, me_gx)
 
-    def xy_peer(k):
-        to = (me_xy + k) % xy_count
-        return ((to // Y_RING) * 2 + me_core, me_z * Y_RING + to % Y_RING)
+    def hops(offset, count):
+        return min(offset, count - offset)
+
+    xy_offsets = sorted(
+        ((dx, dy) for dx in range(x_count) for dy in range(Y_RING) if (dx, dy) != (0, 0)),
+        key=lambda at: -(hops(at[0], x_count) + hops(at[1], Y_RING)),
+    )
+    z_offsets = sorted(range(1, z_count), key=lambda at: -hops(at, z_count))
+
+    def xy_place(at):
+        return (me_x + at[0]) % x_count, (me_y + at[1]) % Y_RING
+
+    def xy_peer(at):
+        x, y = xy_place(at)
+        return (x * 2 + me_core, me_z * Y_RING + y)
+
+    def xy_index(at):
+        x, y = xy_place(at)
+        return x * Y_RING + y
 
     def z_peer(k):
         return (me_dp, ((me_z + k) % z_count) * Y_RING + me_y)
@@ -121,13 +138,13 @@
                 low = plane * TRIPLE + CH
                 field[s, low : low + CH, 0:SPAN] = jnp.zeros((CH, SPAN), BF16)
                 field[s, low : low + CH, PADDED - SPAN : PADDED] = jnp.zeros((CH, SPAN), BF16)
-    for at in range(2):
+    for at in range(6):
         part[at, :, 0:SPAN] = jnp.zeros((TRIPLE, SPAN), F32)
         part[at, :, PADDED - SPAN : PADDED] = jnp.zeros((TRIPLE, SPAN), F32)
 
     barrier = pltpu.get_barrier_semaphore()
     peers = [left, right, sibling]
-    peers += [xy_peer(k) for k in range(1, xy_count)]
+    peers += [xy_peer(at) for at in xy_offsets]
     peers += [z_peer(k) for k in range(1, z_count)]
     for peer in peers:
         pl.semaphore_signal(barrier, inc=1, device_id=peer, device_id_type=MESH)
@@ -228,14 +245,17 @@
 
     loads[6].wait()
     loads[7].wait()
-    for b in range(3):
-        for source, target in ((one, w_one), (two, w_two)):
+    def turned_weights(source, target):
+        for b in range(3):
             stacked = jnp.concatenate(
                 [source[(a * 3 + b) * 3 + e] for a in range(3) for e in range(3)], axis=0
             )
             target[b * CH : (b + 1) * CH, :] = lax.dot_general(
                 eye, stacked, NT, preferred_element_type=F32
             ).astype(BF16)
+
+    turned_weights(one, w_one)
+    for b in range(3):
         flat = jnp.concatenate(
             [
                 lax.dot_general(
@@ -249,6 +269,9 @@
         w_back[b * CH : (b + 1) * CH, :] = lax.dot_general(
             eye, flat, NT, preferred_element_type=F32
         ).astype(BF16)
+        w_tail[b * CH : (b + 1) * CH, :] = lax.dot_general(
+            eye, flat[TRIPLE:], NT, preferred_element_type=F32
+        ).astype(BF16)
 
     def products(field, weights, s, x, at):
         part[at, :, SPAN : SPAN + CELLS] = jnp.dot(
@@ -270,8 +293,26 @@
             factor[s, x, :, z * SPAN : (z + 1) * SPAN] = q * (1.0 + pre * (1.0 - q))
             put(hid3, s, x + 1, z, pre * q, 1)
 
+    def backward_own(s, x, at):
+        inner = slice(SPAN, SPAN + CELLS)
+        weights, low = (w_tail[...], TRIPLE) if x == 0 else (w_back[:, 0 : 2 * TRIPLE], 3 * TRIPLE)
+        part[at, :, inner] = jnp.dot(
+            weights, cot3[s, low : low + 2 * TRIPLE, inner], preferred_element_type=F32
+        )
+
+    def backward_rest(s, x, at):
+        inner = slice(SPAN, SPAN + CELLS)
+        weights, low = (w_back[:, 0:TRIPLE], 0) if x == 0 else (w_back[:, 2 * TRIPLE :], 5 * TRIPLE)
+        part[at, :, inner] += jnp.dot(
+            weights, cot3[s, low : low + TRIPLE, inner], preferred_element_type=F32
+        )
+        to_d_pre(s, x, at)
+
     def backward(s, x, at):
         products(cot3, w_back, s, x, at)
+        to_d_pre(s, x, at)
+
+    def to_d_pre(s, x, at):
         for z in range(DEPTH):
             d_pre = summed(z, -1, at) * factor[s, x, :, z * SPAN : (z + 1) * SPAN]
             before, after = shifted(d_pre)
@@ -295,17 +336,19 @@
     inner = [(s, x) for s in range(SAMPLES) for x in range(1, PLANES - 1)]
     edges = [(s, x) for s in range(SAMPLES) for x in (0, PLANES - 1)]
 
-    def gradient(total, taps_of, others_of, places):
+    def gradient(a, taps_of, others_of, places):
         taps = jnp.concatenate(
             [
                 jnp.concatenate([taps_of(s, x, a, b) for s, x in places], axis=1)
-                for a in range(3)
                 for b in range(3)
             ],
             axis=0,
         )
         others = jnp.concatenate([others_of(s, x) for s, x in places], axis=1)
-        return total + lax.dot_general(taps, others, NT, preferred_element_type=F32)
+        return lax.dot_general(taps, others, NT, preferred_element_type=F32)
+
+    def tap_rows(a):
+        return slice(a * TRIPLE, (a + 1) * TRIPLE)
 
     def base_taps(s, x, a, b):
         low = (x + a) * TRIPLE + CH
@@ -371,34 +414,33 @@
         total = packed[g, my_half(), :].astype(F32) + got_core[g].astype(F32)
         mine[g] = total.astype(BF16)
         copies = []
-        for k in range(1, xy_count):
-            src = mine.at[g, rows(((me_xy + k) % xy_count) * chunk, chunk)]
-            copies.append(remote(src, got_xy.at[g, k - 1], sum_xy, (g, k - 1), xy_peer(k)))
+        for k, at in enumerate(xy_offsets):
+            src = mine.at[g, rows(xy_index(at) * chunk, chunk)]
+            copies.append(remote(src, got_xy.at[g, k], sum_xy, (g, k), xy_peer(at)))
         return start(copies)
 
-    def spread_z(waits):
-        for g, copies in enumerate(waits):
-            arrived(copies)
-            total = mine[g, rows(me_xy * chunk, chunk), :].astype(F32)
-            for k in range(xy_count - 1):
-                total = total + got_xy[g, k].astype(F32)
-            all_z[me_z, g] = total.astype(BF16)
-        own = all_z.at[me_z]
-        return start([remote(own, own, sum_z, k - 1, z_peer(k)) for k in range(1, z_count)])
-
-    def gather_xy(copies):
+    def spread_z(g, copies):
         arrived(copies)
-        total = all_z[0].astype(F32)
+        total = mine[g, rows(me_xy * chunk, chunk), :].astype(F32)
+        for k in range(xy_count - 1):
+            total = total + got_xy[g, k].astype(F32)
+        all_z[g, me_z] = total.astype(BF16)
+        own = all_z.at[g, me_z]
+        return start([remote(own, own, sum_z, (g, k - 1), z_peer(k)) for k in z_offsets])
+
+    def gather_xy(g, copies):
+        arrived(copies)
+        total = all_z[g, 0].astype(F32)
         for k in range(1, z_count):
-            total = total + all_z[k].astype(F32)
-        full[:, my_chunk(), :] = (total * scale).astype(BF16)
-        own = full.at[:, my_chunk()]
-        return start([remote(own, own, back_xy, k - 1, xy_peer(k)) for k in range(1, xy_count)])
-
-    def gather_core(copies):
+            total = total + all_z[g, k].astype(F32)
+        full[g, my_chunk(), :] = (total * scale).astype(BF16)
+        own = full.at[g, my_chunk()]
+        return start([remote(own, own, back_xy, (g, k), xy_peer(at)) for k, at in enumerate(xy_offsets)])
+
+    def gather_core(g, copies):
         arrived(copies)
-        own = full.at[:, my_half()]
-        return start([remote(own, own, back_core, 0, sibling)])
+        own = full.at[g, my_half()]
+        return start([remote(own, own, back_core, g, sibling)])
 
     def give_back(s):
         def step(c, carry):
@@ -410,7 +452,8 @@
 
     planes_of(first_layer, inner)
     planes_of(backward, inner)
-    acc[1] = gradient(0.0, cot_taps, hidden_of, inner)
+    for a in range(3):
+        acc[1, tap_rows(a)] = gradient(a, cot_taps, hidden_of, inner)
     for s in range(SAMPLES):
         for copy in halos[0][s]:
             copy.wait_recv()
@@ -420,32 +463,49 @@
     for s in range(SAMPLES):
         for copy in halos[2][s]:
             copy.start()
-    acc[0] = gradient(0.0, base_taps, d_pre_of, inner)
+    for a in range(3):
+        acc[0, tap_rows(a)] = gradient(a, base_taps, d_pre_of, inner)
+    own_side = ([(s, 0) for s in range(SAMPLES)], edges, [(s, PLANES - 1) for s in range(SAMPLES)])
+    for a in range(3):
+        acc[1, tap_rows(a)] += gradient(a, cot_taps, hidden_of, own_side[a])
+    for i, (s, x) in enumerate(edges):
+        backward_own(s, x, 2 + i)
+    turned_weights(two, w_two)
     for s in range(SAMPLES):
         for copy in halos[1][s]:
             copy.wait_recv()
+    for a in (0, 2):
+        acc[1, tap_rows(a)] += gradient(a, cot_taps, hidden_of, own_side[2 - a])
+    pack(1, acc[1])
+    core_one = to_sibling(1)
     for s in range(SAMPLES):
         halo_shifts(cot3, s, -1)
-    planes_of(backward, edges)
-    pack(0, gradient(acc[0], base_taps, d_pre_of, edges))
+    for i, (s, x) in enumerate(edges):
+        backward_rest(s, x, 2 + i)
+    xy_one = spread_xy(1, core_one)
+    for a in range(3):
+        acc[0, tap_rows(a)] += gradient(a, base_taps, d_pre_of, edges)
+    pack(0, acc[0])
     core_zero = to_sibling(0)
-    pack(1, gradient(acc[1], cot_taps, hidden_of, edges))
-    core_one = to_sibling(1)
+    planes_of(second_layer, inner[:2])
     xy_zero = spread_xy(0, core_zero)
-    planes_of(second_layer, inner)
-    xy_one = spread_xy(1, core_one)
+    planes_of(second_layer, inner[2:])
+    z_one = spread_z(1, xy_one)
     for s in range(SAMPLES):
         for copy in halos[2][s]:
             copy.wait_recv()
     for s in range(SAMPLES):
         halo_shifts(hid3, s, 1)
     planes_of(second_layer, edges)
-    waits = spread_z((xy_zero, xy_one))
+    z_zero = spread_z(0, xy_zero)
     give_back(0)
     give_back(1)
-    waits = gather_xy(waits)
-    waits = gather_core(waits)
-    arrived(waits)
+    full_one = gather_xy(1, z_one)
+    full_zero = gather_xy(0, z_zero)
+    last_one = gather_core(1, full_one)
+    last_zero = gather_core(0, full_zero)
+    arrived(last_one)
+    arrived(last_zero)
 
     for field in halos:
         for side in field:
@@ -511,23 +571,24 @@
             field,
             pltpu.VMEM((SAMPLES, PLANES * TRIPLE, CELLS), BF16),
             pltpu.VMEM((SAMPLES, PLANES, CH, CELLS), F32),
-            pltpu.VMEM((2, TRIPLE, PADDED), F32),
+            pltpu.VMEM((6, TRIPLE, PADDED), F32),
             pltpu.VMEM((TRIPLE, 3 * TRIPLE), BF16),
             pltpu.VMEM((TRIPLE, 3 * TRIPLE), BF16),
             pltpu.VMEM((TRIPLE, 3 * TRIPLE), BF16),
+            pltpu.VMEM((TRIPLE, 2 * TRIPLE), BF16),
             pltpu.VMEM((2, 9 * CH, TRIPLE), F32),
             pltpu.VMEM((2, PACKED, SPAN), BF16),
             pltpu.VMEM((2, half, SPAN), BF16),
             pltpu.VMEM((2, half, SPAN), BF16),
             pltpu.VMEM((2, xy_count - 1, chunk, SPAN), BF16),
-            pltpu.VMEM((z_count, 2, chunk, SPAN), BF16),
+            pltpu.VMEM((2, z_count, chunk, SPAN), BF16),
             dma((8,)),
             dma((3, SAMPLES, 2)),
             dma((3, SAMPLES, 2)),
         ]
         + [
             dma(shape)
-            for shape in ((2,), (2, xy_count - 1), (max(z_count - 1, 1),), (xy_count - 1,), (1,))
+            for shape in ((2,), (2, xy_count - 1), (2, max(z_count - 1, 1)), (2, xy_count - 1), (2,))
             for _ in range(2)
         ],
         compiler_params=pltpu.CompilerParams(

time: 56.5 us -> 51.4 us (0.910)
  Pallas kernels: 55.6 us -> 50.5 us
    pallas_call x1, Pallas kernels: 54 us -> 48.9 us  [on_device(): pl.pallas_call(functools.partial(body, dp_count, z_count, 1.0 / math.sqrt...]
where the time goes in v4:
time: 51.4 us; the launch traced here: 51.3 us
  Pallas kernels  50.5 us (98%)
  between operations  0.82 us (2%)
    pallas_call x1, Pallas kernels, on_device(): pl.pallas_call(functools.partial(body, dp_count, z_count, 1.0 / math.sqrt...  48.9 us
    pallas_call x1, Pallas kernels, on_device(): pl.pallas_call(finish, out_shape=(jax.ShapeDtypeStruct(flat, BF16), jax.S...  1.58 us

profile of v4, /device:TPU:1, one launch (start us, length us, event | category | flops | bytes accessed | tf_op | source)
XLA Modules:
  0.0 51.3 jit_solution(4115375083992043449)
XLA Ops:
  0.6 48.9 %surrogate.1 = (bf16[2,64,32,128]{3,2,1,0:T(8,128)(2,1)S(1)}, bf16[2,1024,128]{2,1,0:T(8,128)(2,1)S(1)}) custom-call(bf16[2,64,32,128]{3,2,1,0:T(8,128)(2,1)} %bitcast.7, s32[2,4,8,128]{3,2,1,0:T(8,128)} %labels_hbm.1, f32[8,64]{1,0:T(8,128)} %emb_hbm.1, bf16[27,64,64]{2,1,0:T(8,128)(2,1)} %bitcast.9, bf16[27,64,64]{2,1,0:T(8,128)(2,1)} %bitcast.10, ...), custom_call_target="tpu_custom_call" | custom-call | tf_op jit(solution)/shard_map/surrogate/pallas_call | solution.py:556
  49.6 1.6 %finish.1 = (bf16[2,64,32,128]{3,2,1,0:T(8,128)(2,1)}, f32[27,64,64]{2,1,0:T(8,128)}, f32[27,64,64]{2,1,0:T(8,128)}) custom-call(bf16[2,64,32,128]{3,2,1,0:T(8,128)(2,1)S(1)} %get-tuple-element.8.held, bf16[2,1024,128]{2,1,0:T(8,128)(2,1)S(1)} %get-tuple-element.9.sums), custom_call_target="tpu_custom_call" | custom-call | tf_op jit(solution)/shard_map/finish/pallas_call | solution.py:606

commit v5 on v4

--- a/solution.py
+++ b/solution.py
@@ -48,6 +48,7 @@
     cot_hbm,
     held,
     full,
+    spread_two,
     feat,
     cot,
     labels,
@@ -229,19 +230,18 @@
     for s in range(SAMPLES):
         loads[2 + s].wait()
         widen(feat, s)
-        for x in range(PLANES):
+        for x in (0, PLANES - 1):
             base_plane(s, x)
         if s == 0:
             pl.semaphore_wait(barrier, len(peers))
         for copy in halos[0][s]:
             copy.start()
     for s in range(SAMPLES):
+        for x in range(1, PLANES - 1):
+            base_plane(s, x)
+    for s in range(SAMPLES):
         loads[4 + s].wait()
         widen(cot, s)
-        for x in range(PLANES):
-            cot_plane(s, x)
-        for copy in halos[1][s]:
-            copy.start()
 
     loads[6].wait()
     loads[7].wait()
@@ -287,6 +287,9 @@
 
     def first_layer(s, x, at):
         products(base3, w_one, s, x, at)
+        to_hidden(s, x, at)
+
+    def to_hidden(s, x, at):
         for z in range(DEPTH):
             pre = summed(z, 1, at)
             q = jax.nn.sigmoid(pre)
@@ -387,13 +390,14 @@
             device_id_type=MESH,
         )
 
-    sent = []
-
     def start(copies):
         for copy in copies:
             copy.start()
-        sent.extend(copies)
         return copies
+
+    def left_device(copies):
+        for copy in copies:
+            copy.wait_send()
 
     def arrived(copies):
         for copy in copies:
@@ -450,13 +454,24 @@
 
         lax.fori_loop(0, CH // 8, step, 0)
 
-    planes_of(first_layer, inner)
+    for s in range(SAMPLES):
+        products(base3, w_one, s, 1, 0)
+        cot_plane(s, 0)
+        cot_plane(s, PLANES - 1)
+        products(base3, w_one, s, 2, 1)
+        to_hidden(s, 1, 0)
+        cot_plane(s, 1)
+        cot_plane(s, 2)
+        to_hidden(s, 2, 1)
+        for copy in halos[1][s]:
+            copy.start()
     planes_of(backward, inner)
-    for a in range(3):
+    for a in (0, 1):
         acc[1, tap_rows(a)] = gradient(a, cot_taps, hidden_of, inner)
     for s in range(SAMPLES):
         for copy in halos[0][s]:
             copy.wait_recv()
+    acc[1, tap_rows(2)] = gradient(2, cot_taps, hidden_of, inner)
     for s in range(SAMPLES):
         halo_shifts(base3, s, 1)
     planes_of(first_layer, edges)
@@ -476,10 +491,10 @@
             copy.wait_recv()
     for a in (0, 2):
         acc[1, tap_rows(a)] += gradient(a, cot_taps, hidden_of, own_side[2 - a])
+    for s in range(SAMPLES):
+        halo_shifts(cot3, s, -1)
     pack(1, acc[1])
     core_one = to_sibling(1)
-    for s in range(SAMPLES):
-        halo_shifts(cot3, s, -1)
     for i, (s, x) in enumerate(edges):
         backward_rest(s, x, 2 + i)
     xy_one = spread_xy(1, core_one)
@@ -500,47 +515,61 @@
     z_zero = spread_z(0, xy_zero)
     give_back(0)
     give_back(1)
+    for field in halos:
+        for side in field:
+            left_device(side)
+    left_device(core_one + core_zero + xy_one + xy_zero)
     full_one = gather_xy(1, z_one)
     full_zero = gather_xy(0, z_zero)
+    left_device(z_one + z_zero)
     last_one = gather_core(1, full_one)
+    left_device(full_one)
     last_zero = gather_core(0, full_zero)
+    left_device(full_zero)
     arrived(last_one)
+    spread_turned(full, spread_two)
+    left_device(last_one)
     arrived(last_zero)
-
-    for field in halos:
-        for side in field:
-            for copy in side:
-                copy.wait_send()
-    for copy in sent:
-        copy.wait_send()
-
-
-def finish(held, sums, out_hbm, grad_one, grad_two, spread, sems):
-    copies = [pltpu.make_async_copy(held, out_hbm, sems.at[0])]
-    copies[0].start()
+    left_device(last_zero)
+
+
+def spread_turned(sums, target):
     eye = (
         lax.broadcasted_iota(jnp.int32, (SPAN, SPAN), 0)
         == lax.broadcasted_iota(jnp.int32, (SPAN, SPAN), 1)
     ).astype(BF16)
-    for g, target in enumerate((grad_one, grad_two)):
-        for piece in range(14):
-            block = sums[g, piece * CH : (piece + 1) * CH, :]
-            if g == 0:
-                block = block.astype(F32)
-                pair = (block[:, 0:CH], block[:, CH:])
-            else:
-                block = lax.dot_general(eye, block, NT, preferred_element_type=F32)
-                pair = (block[0:CH], block[CH:])
-            if piece < 9:
-                spread[g, piece * 3] = pair[0]
-                spread[g, piece * 3 + 1] = pair[1]
-            else:
-                tap = 2 * (piece - 9)
-                spread[g, tap * 3 + 2] = pair[0]
-                if tap < 8:
-                    spread[g, tap * 3 + 5] = pair[1]
-        copies.append(pltpu.make_async_copy(spread.at[g], target, sems.at[1 + g]))
-        copies[-1].start()
+    for piece in range(14):
+        block = sums[1, piece * CH : (piece + 1) * CH, :]
+        block = lax.dot_general(eye, block, NT, preferred_element_type=F32)
+        if piece < 9:
+            target[piece * 3] = block[0:CH]
+            target[piece * 3 + 1] = block[CH:]
+        else:
+            tap = 2 * (piece - 9)
+            target[tap * 3 + 2] = block[0:CH]
+            if tap < 8:
+                target[tap * 3 + 5] = block[CH:]
+
+
+def finish(held, sums, spread_two, out_hbm, grad_one, grad_two, spread, sems):
+    copies = [
+        pltpu.make_async_copy(held, out_hbm, sems.at[0]),
+        pltpu.make_async_copy(spread_two, grad_two, sems.at[1]),
+    ]
+    for copy in copies:
+        copy.start()
+    for piece in range(14):
+        block = sums[0, piece * CH : (piece + 1) * CH, :].astype(F32)
+        if piece < 9:
+            spread[piece * 3] = block[:, 0:CH]
+            spread[piece * 3 + 1] = block[:, CH:]
+        else:
+            tap = 2 * (piece - 9)
+            spread[tap * 3 + 2] = block[:, 0:CH]
+            if tap < 8:
+                spread[tap * 3 + 5] = block[:, CH:]
+    copies.append(pltpu.make_async_copy(spread, grad_one, sems.at[2]))
+    copies[-1].start()
     for copy in copies:
         copy.wait()
 
@@ -553,11 +582,15 @@
     flat = (SAMPLES, CH, PLANES * DEPTH, SPAN)
     dma = pltpu.SemaphoreType.DMA
     field = pltpu.VMEM((SAMPLES, (PLANES + 2) * TRIPLE, PADDED), BF16)
-    held, sums = pl.pallas_call(
+    held, sums, spread_two = pl.pallas_call(
         functools.partial(body, dp_count, z_count, 1.0 / math.sqrt(count)),
-        out_shape=(pltpu.VMEM(flat, BF16), pltpu.VMEM((2, PACKED, SPAN), BF16)),
+        out_shape=(
+            pltpu.VMEM(flat, BF16),
+            pltpu.VMEM((2, PACKED, SPAN), BF16),
+            pltpu.VMEM((27, CH, CH), F32),
+        ),
         in_specs=[pl.BlockSpec(memory_space=pltpu.HBM)] * 6,
-        out_specs=(pl.BlockSpec(memory_space=pltpu.VMEM),) * 2,
+        out_specs=(pl.BlockSpec(memory_space=pltpu.VMEM),) * 3,
         scratch_shapes=[
             pltpu.VMEM(flat, BF16),
             pltpu.VMEM(flat, BF16),
@@ -610,12 +643,12 @@
             jax.ShapeDtypeStruct((27, CH, CH), F32),
             jax.ShapeDtypeStruct((27, CH, CH), F32),
         ),
-        in_specs=[pl.BlockSpec(memory_space=pltpu.VMEM)] * 2,
+        in_specs=[pl.BlockSpec(memory_space=pltpu.VMEM)] * 3,
         out_specs=(pl.BlockSpec(memory_space=pltpu.HBM),) * 3,
-        scratch_shapes=[pltpu.VMEM((2, 27, CH, CH), F32), dma((3,))],
+        scratch_shapes=[pltpu.VMEM((27, CH, CH), F32), dma((3,))],
         compiler_params=pltpu.CompilerParams(vmem_limit_bytes=16 * 1024 * 1024),
         name="finish",
-    )(held, sums)
+    )(held, sums, spread_two)
     taps = (3, 3, 3, CH, CH)
     return output.reshape(features.shape), grad_one.reshape(taps), grad_two.reshape(taps)
 

time: 51.4 us -> 51.3 us (level)
  no operation moved by 1% of the time
where the time goes in v5:
time: 51.3 us; the launch traced here: 51.2 us
  Pallas kernels  50.4 us (98%)
  between operations  0.82 us (2%)
    pallas_call x1, Pallas kernels, on_device(): pl.pallas_call(functools.partial(body, dp_count, z_count, 1.0 / math.sqrt...  48.8 us
    pallas_call x1, Pallas kernels, on_device(): pl.pallas_call(finish, out_shape=(jax.ShapeDtypeStruct(flat, BF16), jax.S...  1.58 us

profile of v5, /device:TPU:1, one launch (start us, length us, event | category | flops | bytes accessed | tf_op | source)
XLA Modules:
  0.0 51.2 jit_solution(11640341902804043861)
XLA Ops:
  0.6 48.8 %surrogate.1 = (bf16[2,64,32,128]{3,2,1,0:T(8,128)(2,1)S(1)}, bf16[2,1024,128]{2,1,0:T(8,128)(2,1)S(1)}, f32[27,64,64]{2,1,0:T(8,128)S(1)}) custom-call(bf16[2,64,32,128]{3,2,1,0:T(8,128)(2,1)} %bitcast.7, s32[2,4,8,128]{3,2,1,0:T(8,128)} %labels_hbm.1, f32[8,64]{1,0:T(8,128)} %emb_hbm.1, bf16[27,64,64]{2,1,0:T(8,128)(2,1)} %bitcast.9, ...), custom_call_target="tpu_custom_call" | custom-call | tf_op jit(solution)/shard_map/surrogate/pallas_call | solution.py:585
  49.5 1.6 %finish.1 = (bf16[2,64,32,128]{3,2,1,0:T(8,128)(2,1)}, f32[27,64,64]{2,1,0:T(8,128)}, f32[27,64,64]{2,1,0:T(8,128)}) custom-call(bf16[2,64,32,128]{3,2,1,0:T(8,128)(2,1)S(1)} %get-tuple-element.9.held, bf16[2,1024,128]{2,1,0:T(8,128)(2,1)S(1)} %get-tuple-element.10.sums, f32[27,64,64]{2,1,0:T(8,128)S(1)} %get-tuple-element.11.spread_two), custom_call_target="tpu_custom_call" | custom-call | tf_op jit(solution)/shard_map/finish/pallas_call | solution.py:639
